TPU v7x, 256 devices: a whole 4x4x8 slice. The times are simulated.
256 devices in a mesh: expert: 32 (over y, x, core), tensor: 8 (over z).
Axes of the slice: x: 4, y: 4, z: 8, core: 2. Of those that a mesh axis runs over, the one named last changes fastest.
Arguments:
- tokens: bfloat16 [4096, 3584], P('expert', 'tensor'), may hold values from -6 to 6
- cotangent: bfloat16 [4096, 3584], P('expert', 'tensor'), may hold values from -3 to 3
- routes: int32 [4096, 2], P('expert'), may hold values from 0 to 15, all different within a row; in each aligned block of 128 rows (0 to 127, 128 to 255, ...) at most 20 rows name the same one
- route_weights: float32 [4096, 2], P('expert'), may hold values from 0.1 to 1
- dense_gate: bfloat16 [8, 608, 3584], P('tensor', 'expert'), may hold values from -0.09375 to 0.09375
- dense_up: bfloat16 [8, 608, 3584], P('tensor', 'expert'), may hold values from -0.09375 to 0.09375
- dense_down: bfloat16 [8, 608, 3584], P('tensor', 'expert'), may hold values from -0.078125 to 0.078125
- expert_gate: bfloat16 [38912, 3584], P(('expert', 'tensor')), may hold values from -0.09375 to 0.09375
- expert_up: bfloat16 [38912, 3584], P(('expert', 'tensor')), may hold values from -0.09375 to 0.09375
- expert_down: bfloat16 [38912, 3584], P(('expert', 'tensor')), may hold values from -0.125 to 0.125
Outputs:
- grad_input: bfloat16 [4096, 3584], P('expert', 'tensor')
- grad_expert_gate: bfloat16 [38912, 3584], P(('expert', 'tensor'))
- grad_expert_up: bfloat16 [38912, 3584], P(('expert', 'tensor'))
- grad_expert_down: bfloat16 [38912, 3584], P(('expert', 'tensor'))
Inputs may be any that keep to these rules, and one draw needn't show every extreme that they name: `routes`: among the tokens of one owner (aligned blocks of 128 tokens) each expert is named at most 20 times; a token names 2 different experts.
All inputs are finite; a program needn't handle non-finite values.
Results may differ from a plain program's by a relative error of at most 0.019.
Values may be sent and summed in bfloat16 or wider, within the bound.
A program may use at most 256 MiB of HBM per device.

v0:
```python
import jax
import jax.numpy as jnp
from jax import lax
from jax.sharding import PartitionSpec as P

GROUP = 2


def dot_rows(left, right):
    return lax.dot_general(
        left, right, (((1,), (1,)), ((), ())), preferred_element_type=jnp.float32
    )


def dot_cols(left, right):
    return lax.dot_general(
        left, right, (((0,), (0,)), ((), ())), preferred_element_type=jnp.float32
    )


def rounded(value):
    narrow = value.astype(jnp.bfloat16)
    narrow = lax.optimization_barrier(narrow)
    return narrow.astype(jnp.float32)


def swiglu_grads(gate_pre, up_pre, grad_hidden):
    sigmoid_gate = jax.nn.sigmoid(gate_pre)
    silu_gate = gate_pre * sigmoid_gate
    slopes = sigmoid_gate * (1.0 + gate_pre * (1.0 - sigmoid_gate))
    grad_gate = (grad_hidden * up_pre * slopes).astype(jnp.bfloat16)
    grad_up = (grad_hidden * silu_gate).astype(jnp.bfloat16)
    return (silu_gate, grad_gate, grad_up)


def slot_ranks(flat_ids, count):
    onehot = (flat_ids[:, None] == jnp.arange(count, dtype=jnp.int32)[None, :]).astype(jnp.int32)
    before = jnp.cumsum(onehot, axis=0) - onehot
    return jnp.sum(before * onehot, axis=1)


def place_rows(placing, copies, experts_here, capacity):
    packed = jnp.dot(placing, copies, preferred_element_type=jnp.float32).astype(jnp.bfloat16)
    return packed.reshape(experts_here, capacity, copies.shape[1])


def pack_slots(placing, copies, weighted, experts_here, capacity):
    slot_in = place_rows(placing, copies, experts_here, capacity)
    slot_grad = place_rows(placing, weighted, experts_here, capacity)
    return (jnp.repeat(slot_in, GROUP, axis=0), jnp.repeat(slot_grad, GROUP, axis=0))


def owner_rows(returned, slots, experts_here, capacity, tok_rows, top_count):
    width = returned.shape[2]
    grouped = returned.reshape(experts_here, GROUP, capacity, width).sum(axis=1)
    flat_sums = grouped.reshape(experts_here * capacity, width)
    return flat_sums[slots].reshape(tok_rows, top_count, width).sum(axis=1)


def body(
    tokens,
    cotangent,
    routes,
    route_weights,
    dense_gate,
    dense_up,
    dense_down,
    expert_gate,
    expert_up,
    expert_down,
):
    tok_rows = tokens.shape[0]
    top_count = routes.shape[1]
    groups = lax.axis_size("expert")
    experts_here = groups // GROUP
    capacity = min(tok_rows, 5 * tok_rows * top_count // (4 * experts_here))
    full_tokens, full_cot = (
        lax.all_gather(tokens, "tensor", axis=1, tiled=True),
        lax.all_gather(cotangent, "tensor", axis=1, tiled=True),
    )
    feature_count = dense_gate.shape[2]
    rows_gate = lax.all_gather(dense_gate, "expert", axis=1, tiled=True).reshape(-1, feature_count)
    rows_up = lax.all_gather(dense_up, "expert", axis=1, tiled=True).reshape(-1, feature_count)
    rows_down = lax.all_gather(dense_down, "expert", axis=1, tiled=True).reshape(-1, feature_count)
    gate_pre = dot_rows(full_tokens, rows_gate)
    up_pre = dot_rows(full_tokens, rows_up)
    grad_hidden = dot_rows(full_cot, rows_down)
    silu_gate, grad_gate, grad_up = swiglu_grads(gate_pre, up_pre, grad_hidden)
    dense_term = rounded(
        jnp.dot(grad_gate, rows_gate, preferred_element_type=jnp.float32)
        + jnp.dot(grad_up, rows_up, preferred_element_type=jnp.float32)
    )
    flat_ids = routes.reshape(-1)
    ranks = slot_ranks(flat_ids, experts_here)
    slots = flat_ids * capacity + ranks
    placing = (
        slots[None, :] == jnp.arange(experts_here * capacity, dtype=jnp.int32)[:, None]
    ).astype(jnp.bfloat16)
    flat_weights = route_weights.reshape(-1)[:, None]
    copies = jnp.repeat(tokens, top_count, axis=0)
    weighted = (jnp.repeat(cotangent, top_count, axis=0).astype(jnp.float32) * flat_weights).astype(
        jnp.bfloat16
    )
    send_tokens, send_cot = pack_slots(placing, copies, weighted, experts_here, capacity)
    recv_tokens, recv_cot = (
        lax.all_to_all(send_tokens, "expert", split_axis=0, concat_axis=0, tiled=True),
        lax.all_to_all(send_cot, "expert", split_axis=0, concat_axis=0, tiled=True),
    )
    slot_tokens, slot_cot = (
        lax.all_gather(recv_tokens, "tensor", axis=2, tiled=True),
        lax.all_gather(recv_cot, "tensor", axis=2, tiled=True),
    )
    width = slot_tokens.shape[2]
    rows_in = slot_tokens.reshape(groups * capacity, width)
    rows_cot = slot_cot.reshape(groups * capacity, width)
    pre_gate = dot_rows(rows_in, expert_gate)
    pre_up = dot_rows(rows_in, expert_up)
    hidden_grad = dot_rows(rows_cot, expert_down)
    silu_pre, expert_grad_gate, expert_grad_up = swiglu_grads(pre_gate, pre_up, hidden_grad)
    hidden = (silu_pre * pre_up).astype(jnp.bfloat16)
    grad_down_w = dot_cols(hidden, rows_cot).astype(jnp.bfloat16)
    grad_gate_w = dot_cols(expert_grad_gate, rows_in).astype(jnp.bfloat16)
    grad_up_w = dot_cols(expert_grad_up, rows_in).astype(jnp.bfloat16)
    slot_term = rounded(
        jnp.dot(expert_grad_gate, expert_gate, preferred_element_type=jnp.float32)
        + jnp.dot(expert_grad_up, expert_up, preferred_element_type=jnp.float32)
    )
    partial_sum = lax.psum_scatter(
        slot_term.reshape(groups, capacity, width).astype(jnp.bfloat16),
        "tensor",
        scatter_dimension=2,
        tiled=True,
    ).astype(jnp.float32)
    returned = lax.all_to_all(
        partial_sum.astype(jnp.bfloat16), "expert", split_axis=0, concat_axis=0, tiled=True
    ).astype(partial_sum.dtype)
    expert_in = owner_rows(returned, slots, experts_here, capacity, tok_rows, top_count)
    total = (
        lax.psum_scatter(
            dense_term.astype(jnp.bfloat16), "tensor", scatter_dimension=1, tiled=True
        ).astype(jnp.float32)
        + expert_in
    )
    return (total.astype(jnp.bfloat16), grad_gate_w, grad_up_w, grad_down_w)


def solution(mesh):
    return jax.shard_map(
        body,
        mesh=mesh,
        in_specs=(
            P("expert", "tensor"),
            P("expert", "tensor"),
            P("expert", None),
            P("expert", None),
            P("tensor", "expert", None),
            P("tensor", "expert", None),
            P("tensor", "expert", None),
            P(("expert", "tensor"), None),
            P(("expert", "tensor"), None),
            P(("expert", "tensor"), None),
        ),
        out_specs=(
            P("expert", "tensor"),
            P(("expert", "tensor"), None),
            P(("expert", "tensor"), None),
            P(("expert", "tensor"), None),
        ),
        check_vma=False,
    )
```

profile of v0, /device:TPU:16, one launch (start us, length us, event | category | flops | bytes accessed | tf_op | source)
XLA Modules:
  0.0 773.3 jit_solution(14466907745931425017)
XLA Ops:
  11.1 19.2 %all_to_all.15 = bf16[32,20,448]{2,1,0:T(8,128)(2,1)S(1)} all-to-all(bf16[32,20,448]{2,1,0:T(8,128)(2,1)S(1)} %bitcast.73), channel_id=1, replica_groups=mesh['expert'=32,'tensor'=8] {'expert'}, dimensions={0} | all-to-all | bytes 1146880 | tf_op jit(solution)/shard_map/all_to_all | solution.py:106
  35.2 18.0 %all_to_all.16 = bf16[32,20,448]{2,1,0:T(8,128)(2,1)S(1)} all-to-all(bf16[32,20,448]{2,1,0:T(8,128)(2,1)S(1)} %bitcast.74), channel_id=1, replica_groups=mesh['expert'=32,'tensor'=8] {'expert'}, dimensions={0} | all-to-all | bytes 1146880 | tf_op jit(solution)/shard_map/all_to_all | solution.py:107
  59.7 197.5 %all-gather.14.cloned.1.call-done = bf16[32,20,3584]{0,1,2:T(8,128)(2,1)} async-done(((bf16[32,20,448]{0,1,2:T(8,128)(2,1)}), bf16[32,20,3584]{0,1,2:T(8,128)(2,1)}) %all-gather.14.cloned.1.call-update) | async-done | bytes 4587536 | tf_op jit(solution)/shard_map/all_gather | solution.py:110
  257.2 25.7 %copy.73 = bf16[32,20,3584]{2,1,0:T(8,128)(2,1)} copy(bf16[32,20,3584]{0,1,2:T(8,128)(2,1)} %all-gather.14.cloned.1.call-done) | data formatting | bytes 9175040 | tf_op jit(solution)/shard_map/all_gather | solution.py:110
  282.9 7.3 reshape.122
  290.1 189.4 %all-gather.12.cloned.1.call-done = bf16[32,20,3584]{0,1,2:T(8,128)(2,1)} async-done(((bf16[32,20,448]{0,1,2:T(8,128)(2,1)}), bf16[32,20,3584]{0,1,2:T(8,128)(2,1)}) %all-gather.12.cloned.1.call-update) | async-done | bytes 4587536 | tf_op jit(solution)/shard_map/all_gather | solution.py:111
  479.5 25.6 %copy.68 = bf16[32,20,3584]{2,1,0:T(8,128)(2,1)} copy(bf16[32,20,3584]{0,1,2:T(8,128)(2,1)} %all-gather.12.cloned.1.call-done) | data formatting | bytes 9175040 | tf_op jit(solution)/shard_map/all_gather | solution.py:111
  505.2 7.3 reshape.118
  526.6 7.4 convert_element_type.84
  533.9 27.3 %copy.80 = bf16[32,20,3584]{1,0,2:T(8,128)(2,1)} copy(bf16[32,20,3584]{2,1,0:T(8,128)(2,1)} %convert_element_type.84) | data formatting | bytes 9175040
  561.3 52.1 %reshape.139 = bf16[3584,640]{1,0:T(8,128)(2,1)} reshape(bf16[3584,32,20]{2,1,0:T(8,128)(2,1)} %bitcast.70) | data formatting | bytes 9175040
  614.3 26.7 %all_gather.23 = bf16[128,3584]{0,1:T(8,128)(2,1)S(1)} all-gather(bf16[128,448]{0,1:T(8,128)(2,1)S(1)} %copy-done.5), channel_id=1, replica_groups=mesh['expert'=32,'tensor'=8] {'tensor'}, dimensions={1}, use_global_device_ids=true | all-gather | bytes 1032192 | tf_op jit(solution)/shard_map/all_gather | solution.py:78
  641.0 26.5 %all_gather.21 = bf16[128,3584]{0,1:T(8,128)(2,1)S(1)} all-gather(bf16[128,448]{0,1:T(8,128)(2,1)S(1)} %copy-done.6), channel_id=1, replica_groups=mesh['expert'=32,'tensor'=8] {'tensor'}, dimensions={1}, use_global_device_ids=true | all-gather | bytes 1032192 | tf_op jit(solution)/shard_map/all_gather | solution.py:79
  667.5 5.5 fusion.3
  673.0 5.9 fusion.8
  678.9 9.7 %fusion.1 = f32[128,3584]{1,0:T(8,128)S(1)} fusion(bf16[1,608,3584]{2,0,1:T(2,128)(2,1)} %all-gather.10.cloned.1.call-done, f32[128,608]{0,1:T(8,128)} %fusion.8, bf16[128,3584]{0,1:T(8,128)(2,1)S(1)} %all_gather.23, bf16[1,608,3584]{2,0,1:T(2,128)(2,1)} %all-gather.8.cloned.1.call-done, f32[128,608]{0,1:T(8,128)} %fusion.3), kind=kOutput, calls=%fused_computation.7 | convolution fusion | flops 1116463104 | bytes 12091392 | tf_op jit(solution)/shard_map/dot_general | solution.py:90
  688.7 4.7 fusion
  695.0 4.4 convolution_convert_fusion.1
  699.4 23.6 %reduce-scatter.9.cloned.1.call-done = bf16[448,640]{1,0:T(8,128)(2,1)} async-done(((bf16[3584,640]{1,0:T(8,128)(2,1)}), bf16[448,640]{1,0:T(8,128)(2,1)}) %reduce-scatter.9.cloned.1.call-update) | async-done | bytes 573456
  723.0 10.7 %reshape.140 = bf16[448,32,20]{2,1,0:T(8,128)(2,1)} reshape(bf16[448,640]{1,0:T(8,128)(2,1)} %reduce-scatter.9.cloned.1.call-done) | data formatting | bytes 1146880
  733.6 5.5 copy.81
  739.1 7.5 all-to-all-start.2
  751.0 4.4 convolution_convert_fusion
  755.3 7.2 reduce-scatter.7.cloned.1.call-done
  (101 shorter events, 39.7 us)
Async XLA Ops:
  7.2 505.3 %copy-start = (bf16[152,3584]{1,0:T(8,128)(2,1)S(1)}, bf16[152,3584]{1,0:T(8,128)(2,1)}, u32[]{:S(2)}) copy-start(bf16[152,3584]{1,0:T(8,128)(2,1)} %param.17) | copy-start | bytes 3268612
  7.2 250.0 %all-gather.14.cloned.1.call-start = ((), (), s32[]{:S(2)}) async-start(), calls=%async_computation.9 | async-start | bytes 24772608 | tf_op jit(solution)/shard_map/all_gather | solution.py:110
  11.0 22.7 %copy-start.15 = (f32[128,2]{0,1:T(2,128)S(1)}, f32[128,2]{0,1:T(2,128)}, u32[]{:S(2)}) copy-start(f32[128,2]{0,1:T(2,128)} %param.13) | copy-start | bytes 3076
  11.0 22.9 %copy-start.6 = (bf16[128,448]{0,1:T(8,128)(2,1)S(1)}, bf16[128,448]{0,1:T(8,128)(2,1)}, u32[]{:S(2)}) copy-start(bf16[128,448]{0,1:T(8,128)(2,1)} %param.11) | copy-start | bytes 344068
  33.6 445.9 %all-gather.12.cloned.1.call-start = ((), (), s32[]{:S(2)}) async-start(), calls=%async_computation.8 | async-start | bytes 24772608 | tf_op jit(solution)/shard_map/all_gather | solution.py:111
  35.1 21.4 %copy-start.11 = (bf16[1,19,3584]{2,1,0:T(8,128)(2,1)S(1)}, bf16[1,19,3584]{2,1,0:T(8,128)(2,1)}, u32[]{:S(2)}) copy-start(bf16[1,19,3584]{2,1,0:T(8,128)(2,1)} %param.14) | copy-start | bytes 408580
  35.2 22.3 %copy-start.12 = (bf16[1,19,3584]{2,1,0:T(8,128)(2,1)S(1)}, bf16[1,19,3584]{2,1,0:T(8,128)(2,1)}, u32[]{:S(2)}) copy-start(bf16[1,19,3584]{2,1,0:T(8,128)(2,1)} %param.16) | copy-start | bytes 408580
  35.2 23.3 %copy-start.13 = (bf16[1,19,3584]{2,1,0:T(8,128)(2,1)S(1)}, bf16[1,19,3584]{2,1,0:T(8,128)(2,1)}, u32[]{:S(2)}) copy-start(bf16[1,19,3584]{2,1,0:T(8,128)(2,1)} %param.15) | copy-start | bytes 408580
  56.4 611.1 %all-gather.10.cloned.1.call-start = ((), (), s32[]{:S(2)}) async-start(), calls=%async_computation.7 | async-start | bytes 8988672 | tf_op jit(solution)/shard_map/all_gather | solution.py:82
  57.4 615.6 %all-gather.6.cloned.1.call-start = ((), (), s32[]{:S(2)}) async-start(), calls=%async_computation.5 | async-start | bytes 8988672 | tf_op jit(solution)/shard_map/all_gather | solution.py:84
  58.4 620.5 %all-gather.8.cloned.1.call-start = ((), (), s32[]{:S(2)}) async-start(), calls=%async_computation.6 | async-start | bytes 8988672 | tf_op jit(solution)/shard_map/all_gather | solution.py:83
  59.4 663.5 %reduce-scatter.9.cloned.1.call-start = ((), (), s32[]{:S(2)}) async-start(), calls=%async_computation.11 | async-start | bytes 5160960
  512.5 4.0 copy-start.2
  512.5 4.0 copy-start.4
  516.5 5.1 copy-start.7
  516.5 3.2 copy-start.3
  516.5 3.5 copy-start.16
  520.0 1.6 copy-start.9
  613.4 149.1 %reduce-scatter.7.cloned.1.call-start = ((), (), s32[]{:S(2)}) async-start(), calls=%async_computation.10 | async-start | bytes 1032192
  688.7 6.1 copy-start.14
  739.1 11.9 %copy-start.8 = (f32[640,152]{0,1:T(8,128)S(1)}, f32[640,152]{0,1:T(8,128)}, u32[]{:S(2)}) copy-start(f32[640,152]{0,1:T(8,128)} %copy-done.7) | copy-start | bytes 1167364
  739.1 11.9 %copy-start.10 = (f32[640,152]{0,1:T(8,128)S(1)}, f32[640,152]{0,1:T(8,128)}, u32[]{:S(2)}) copy-start(f32[640,152]{0,1:T(8,128)} %copy-done.9) | copy-start | bytes 1167364
  739.1 24.4 %all-to-all-start.2 = ((bf16[32,20,448]{2,1,0:T(8,128)(2,1)}), bf16[32,20,448]{2,1,0:T(8,128)(2,1)S(1)}, u32[]{:S(2)}, u32[]{:S(2)}) async-start(bf16[32,20,448]{2,1,0:T(8,128)(2,1)} %copy.81), calls=%async_computation.2 | async-start | bytes 1572864 | tf_op jit(solution)/shard_map/all_to_all | solution.py:134
  763.5 3.0 copy-start.1
  (1 other events, 0.9 us)
Sparse Core Ops, SparseCore 0:
  33.8 223.3 all-gather.13
  259.0 220.5 all-gather.11
  482.7 57.1 all-gather.9
  542.4 58.3 all-gather.5
  603.2 58.3 all-gather.7
  664.0 58.8 reduce-scatter.8
  725.7 36.7 reduce-scatter.6
where the time goes:
time: 776 us; the launch traced here: 773 us
  waiting for transfers between devices  418 us (54%)
  local copies, waits for them, and re-layouts  189 us (24%)
  blocking collectives  90.5 us (12%)
  matrix products  51.6 us (7%)
  between operations  14.5 us (2%)
  starting transfers between devices  8 us (1%)
    all_gather x1, waiting for transfers between devices, body(): lax.all_gather(recv_tokens, 'tensor', axis=2, tiled=True)  198 us
    all_gather x1, waiting for transfers between devices, body(): lax.all_gather(recv_cot, 'tensor', axis=2, tiled=True)  189 us
    unnamed x47, local copies, waits for them, and re-layouts  106 us
    unnamed x9, waiting for transfers between devices  30.8 us
    all_gather x1, blocking collectives, body(): lax.all_gather(tokens, 'tensor', axis=1, tiled=True)  26.7 us
    all_gather x1, blocking collectives, body(): lax.all_gather(cotangent, 'tensor', axis=1, tiled=True)  26.5 us
    all_gather x1, local copies, waits for them, and re-layouts, body(): lax.all_gather(recv_tokens, 'tensor', axis=2, tiled=True)  25.7 us
    all_gather x1, local copies, waits for them, and re-layouts, body(): lax.all_gather(recv_cot, 'tensor', axis=2, tiled=True)  25.6 us
  transfers between devices with their start and end apart: 8, of which 4 were waited for; matrix products, arithmetic and copies ran while one was open for 30% of the time, Pallas kernels for 0%

commit v1 on v0

v1 whole, which is shorter than its diff:
```python
import jax
import jax.numpy as jnp
from jax import lax
from jax.experimental import pallas as pl
from jax.experimental.pallas import tpu as pltpu
from jax.sharding import PartitionSpec as P

MESH = pl.DeviceIdType.MESH
BF, F32 = jnp.bfloat16, jnp.float32
NT = (((1,), (1,)), ((), ()))
NN = (((1,), (0,)), ((), ()))
ROWS = 19
PAIR = 896
WIDE = 1152
BACK = 4480


def dot(a, b, dims=NN):
    return lax.dot_general(a, b, dims, preferred_element_type=F32)


def iota(shape, dim):
    return lax.broadcasted_iota(jnp.int32, shape, dim)


def onehot(mask):
    return jnp.where(mask, 1.0, 0.0).astype(BF)


def swiglu(gate, up, grad):
    sig = 1.0 / (1.0 + jnp.exp(-gate))
    silu = gate * sig
    slope = sig * (1.0 + gate * (1.0 - sig))
    return silu, (grad * up * slope).astype(BF), (grad * silu).astype(BF)


def kernel(
    mine, other, place_m, place_l, comb_m, comb_l, w_m, w_l, wblk, eg, eu, ed,
    out_x, out_g, out_u, out_d,
    got, packed, shards, lbuf, wall, sib_w, grm, grl, hm, hl, sib_m, sib_l,
    tr, lstack, fsend, frecv, xc, ggt, rs_send, rs_recv,
    p_sem, c_s, c_r, d_s, d_r, m_s, m_r, b_s, b_r, bm_s, bm_r, w_s, w_r,
    g_s, g_r, f_s, f_r, a_s, a_r, r_s, r_r, loc,
):
    i = lax.axis_index("expert")
    z = lax.axis_index("tensor")
    c = lax.rem(i, 2)
    j = lax.div(i, 2)
    y, x = lax.div(j, 4), lax.rem(j, 4)
    sib = i + 1 - 2 * c
    first = (1 - c) * x + c * y
    second = (1 - c) * y + c * x

    def plane(f, s):
        yy = (1 - c) * s + c * f
        xx = (1 - c) * f + c * s
        return ((yy * 4 + xx) * 2 + c, z)

    def shifted(v, s, n):
        return lax.rem(v + s + n, n)

    pending = []

    def send(src, dst, s_sem, r_sem, dev):
        copy = pltpu.make_async_remote_copy(
            src_ref=src, dst_ref=dst, send_sem=s_sem, recv_sem=r_sem,
            device_id=dev, device_id_type=MESH,
        )
        copy.start()
        pending.append(copy)

    def arrived(ref, s_sem, r_sem):
        pltpu.make_async_remote_copy(
            src_ref=ref, dst_ref=ref, send_sem=s_sem, recv_sem=r_sem,
            device_id=(sib, z), device_id_type=MESH,
        ).wait_recv()

    def chip(k):
        xx = lax.rem(x + k % 4, 4)
        yy = lax.rem(y + k // 4, 4)
        return yy * 4 + xx

    def chip_back(k):
        xx = lax.rem(x + 4 - k % 4, 4)
        yy = lax.rem(y + 4 - k // 4, 4)
        return yy * 4 + xx

    barrier = pltpu.get_barrier_semaphore()
    for k in range(1, 16):
        pl.semaphore_signal(barrier, inc=1, device_id=(chip(k) * 2 + c, z), device_id_type=MESH)
    pl.semaphore_signal(barrier, inc=1, device_id=(sib, z), device_id_type=MESH)
    for s in range(1, 8):
        pl.semaphore_signal(barrier, inc=1, device_id=(i, shifted(z, s, 8)), device_id_type=MESH)
    pl.semaphore_wait(barrier, 23)

    even = lax.rem(z, 2) == 0
    partner = z + 1 - 2 * lax.rem(z, 2)
    send(other, got, p_sem.at[0], p_sem.at[1], (i, partner))

    def block(pos, half=None):
        ref = wall.at[c, pos]
        return ref if half is None else ref.at[pl.ds(32 * half, 32), :]

    own_pos = second * 4 + first
    here = pltpu.make_async_copy(wblk, wall.at[c, own_pos], loc.at[0])
    here.start()
    send(wblk, wall.at[c, own_pos], b_s.at[0], b_r.at[0], plane(shifted(first, 1, 4), second))
    send(wblk, wall.at[c, own_pos], b_s.at[1], b_r.at[1], plane(shifted(first, -1, 4), second))

    arrived(got, p_sem.at[0], p_sem.at[1])
    a, b = mine[...], got[...]
    lo = jnp.where(even, a, b)
    hi = jnp.where(even, b, a)
    rows = jnp.concatenate([lo.astype(F32), hi.astype(F32)], axis=1).astype(BF)
    own_xc = (pl.ds(pl.multiple_of(lax.rem(z, 2) * 128, 128), 128),
              pl.ds(pl.multiple_of(lax.div(z, 2) * PAIR, 128), PAIR))
    xc[own_xc] = rows
    packed[:, 0:PAIR] = (dot(place_m[...], rows) * w_m[...]).astype(BF)
    pl_l = place_l[...]
    quarter = (iota((256, 128), 0) >> 2) & 3
    left = jnp.zeros((256, 256), F32)
    for q in range(4):
        sel = jnp.where(quarter == q, pl_l, jnp.zeros_like(pl_l))
        if q < 3:
            left = left + dot(sel, rows[:, 256 * q:256 * q + 256])
        else:
            last = dot(sel, rows[:, 768:896])
    wl = w_l[...]
    packed[:, PAIR:PAIR + 128] = ((left[:, 0:128] + last) * wl).astype(BF)
    packed[:, PAIR + 128:WIDE] = (left[:, 128:256] * wl).astype(BF)

    def rows16(ref, n):
        return ref.at[pl.ds(pl.multiple_of(16 * n, 16), 16), :]

    own_shard = shards.at[z, c]
    for k in range(1, 16):
        to = chip(k)
        send(rows16(packed, to), rows16(own_shard, j), c_s.at[k], c_r.at[k], (to * 2 + c, z))
    keep = pltpu.make_async_copy(rows16(packed, j), rows16(own_shard, j), loc.at[1])
    keep.start()
    here.wait()

    send(wall.at[c, own_pos], wall.at[c, own_pos], bm_s.at[0], bm_r.at[0], (sib, z))
    send(eg, sib_w.at[0], w_s.at[0], w_r.at[0], (sib, z))
    send(eu, sib_w.at[1], w_s.at[1], w_r.at[1], (sib, z))
    before = second * 4 + shifted(first, -1, 4)
    after = second * 4 + shifted(first, 1, 4)
    across = second * 4 + shifted(first, 2, 4)
    arrived(wall.at[c, before], b_s.at[0], b_r.at[0])
    send(block(before, 0), block(before, 0), b_s.at[2], b_r.at[2], plane(shifted(first, 1, 4), second))
    arrived(wall.at[c, after], b_s.at[1], b_r.at[1])
    send(block(after, 1), block(after, 1), b_s.at[3], b_r.at[3], plane(shifted(first, -1, 4), second))

    for k in range(1, 16):
        arrived(rows16(own_shard, chip_back(k)), c_s.at[k], c_r.at[k])
    keep.wait()

    right, left_z = shifted(z, 1, 8), shifted(z, -1, 8)

    def ring_start(view, half, s_sem, r_sem):
        send(view(z), view(z), s_sem.at[0], r_sem.at[0], (i, right))
        send(view(z), view(z), s_sem.at[4], r_sem.at[4], (i, left_z))

    def ring_step(view, half, s_sem, r_sem, s):
        o = shifted(z, -s, 8)
        arrived(view(o), s_sem.at[s - 1], r_sem.at[s - 1])
        part = view(o) if s < 3 else half(o, 0)
        send(part, part, s_sem.at[s], r_sem.at[s], (i, right))
        o = shifted(z, s, 8)
        arrived(view(o), s_sem.at[s + 3], r_sem.at[s + 3])
        part = view(o) if s < 3 else half(o, 1)
        send(part, part, s_sem.at[s + 4], r_sem.at[s + 4], (i, left_z))

    def ring_end(view, half, s_sem, r_sem):
        o = shifted(z, 4, 8)
        arrived(half(o, 0), s_sem.at[3], r_sem.at[3])
        arrived(half(o, 1), s_sem.at[7], r_sem.at[7])

    def shard(o):
        return shards.at[o, c]

    def shard_half(o, h):
        return shards.at[o, c, pl.ds(128 * h, 128), :]

    def mirror(s):
        o = shifted(z, s, 8)
        send(shards.at[o, c], shards.at[o, c], m_s.at[s], m_r.at[s], (sib, z))

    def group(g):
        return wall.at[c, pl.ds(g * 4, 4)]

    def group_half(g, h):
        return wall.at[c, pl.ds(g * 4 + 2 * h, 2)]

    ring_start(shard, shard_half, d_s, d_r)
    arrived(block(across, 0), b_s.at[2], b_r.at[2])
    arrived(block(across, 1), b_s.at[3], b_r.at[3])
    s_up, s_down, s_over = (shifted(second, 1, 4), shifted(second, -1, 4), shifted(second, 2, 4))
    send(group(second), group(second), b_s.at[4], b_r.at[4], plane(first, s_up))
    send(group(second), group(second), b_s.at[5], b_r.at[5], plane(first, s_down))
    mirror(0)
    send(wall.at[c, before], wall.at[c, before], bm_s.at[1], bm_r.at[1], (sib, z))
    send(wall.at[c, after], wall.at[c, after], bm_s.at[2], bm_r.at[2], (sib, z))
    send(wall.at[c, across], wall.at[c, across], bm_s.at[3], bm_r.at[3], (sib, z))

    ring_step(shard, shard_half, d_s, d_r, 1)
    mirror(1)
    mirror(7)
    ring_step(shard, shard_half, d_s, d_r, 2)
    mirror(2)
    mirror(6)
    arrived(group(s_down), b_s.at[4], b_r.at[4])
    send(group_half(s_down, 0), group_half(s_down, 0), b_s.at[6], b_r.at[6], plane(first, s_up))
    send(group(s_down), group(s_down), bm_s.at[4], bm_r.at[4], (sib, z))
    arrived(group(s_up), b_s.at[5], b_r.at[5])
    send(group_half(s_up, 1), group_half(s_up, 1), b_s.at[7], b_r.at[7], plane(first, s_down))
    send(group(s_up), group(s_up), bm_s.at[5], bm_r.at[5], (sib, z))
    ring_step(shard, shard_half, d_s, d_r, 3)

    def xc_view(o):
        return xc.at[pl.ds(pl.multiple_of(lax.rem(o, 2) * 128, 128), 128),
                     pl.ds(pl.multiple_of(lax.div(o, 2) * PAIR, 128), PAIR)]

    def xc_half(o, h):
        return xc.at[pl.ds(pl.multiple_of(lax.rem(o, 2) * 128 + 64 * h, 64), 64),
                     pl.ds(pl.multiple_of(lax.div(o, 2) * PAIR, 128), PAIR)]

    ring_start(xc_view, xc_half, a_s, a_r)
    mirror(3)
    mirror(5)
    ring_end(shard, shard_half, d_s, d_r)
    mirror(4)
    for s in range(8):
        o = shifted(z, s, 8)
        arrived(shards.at[o, 1 - c], m_s.at[s], m_r.at[s])

    r, k_ = iota((256, 256), 0), iota((256, 256), 1)
    unfold = onehot(k_ == ((r >> 2) & 15) * 16 + (r >> 6) * 4 + (r & 3))
    for zz in range(8):
        m, arr = zz // 2, zz % 2
        for cc in range(2):
            flat = dot(unfold, shards[zz, cc, :, PAIR:WIDE]).astype(BF)
            for q in range(4):
                n = 256 if q < 3 else 128
                lbuf[arr, 64 * cc:64 * cc + 64, PAIR * m + 256 * q:PAIR * m + 256 * q + n] = (
                    flat[64 * q:64 * q + 64, 0:n])

    def forward(load_t, load_c):
        gate = jnp.zeros((), F32)
        gate = up = grad = None
        for m in range(4):
            cols = slice(PAIR * m, PAIR * m + PAIR)
            t, ct = load_t(m), load_c(m)
            pg, pu, pd = dot(eg[:, cols], t, NT), dot(eu[:, cols], t, NT), dot(ed[:, cols], ct, NT)
            gate = pg if gate is None else gate + pg
            up = pu if up is None else up + pu
            grad = pd if grad is None else grad + pd
        silu, gg, gu = swiglu(gate, up, grad)
        return (silu * up).astype(BF), gg, gu

    for cc in range(2):
        h, gg, gu = forward(lambda m: shards[2 * m, cc, :, 0:PAIR], lambda m: shards[2 * m + 1, cc, :, 0:PAIR])
        hm[cc] = h
        grm[cc, 0] = gg
        grm[cc, 1] = gu
    h, gg, gu = forward(lambda m: lbuf[0, :, PAIR * m:PAIR * m + PAIR],
                        lambda m: lbuf[1, :, PAIR * m:PAIR * m + PAIR])
    hl[...] = h
    grl[0] = gg
    grl[1] = gu
    send(grm.at[1 - c], sib_m, g_s.at[0], g_r.at[0], (sib, z))
    send(grl, sib_l, g_s.at[1], g_r.at[1], (sib, z))
    ring_step(xc_view, xc_half, a_s, a_r, 1)

    r, k_ = iota((256, 256), 0), iota((256, 256), 1)
    eye = onehot(r == k_)
    pick = onehot(iota((64, 128), 1) == iota((64, 128), 0) + 64 * c)
    arrived(sib_w.at[0], w_s.at[0], w_r.at[0])
    arrived(sib_w.at[1], w_s.at[1], w_r.at[1])
    for n in range(2):
        tr[n, 0:256, :] = dot(eye, grm[c, n], NT).astype(BF)
        tr[n, 256:320, :] = dot(pick, grl[n], NT).astype(BF)
    arrived(sib_m, g_s.at[0], g_r.at[0])
    arrived(sib_l, g_s.at[1], g_r.at[1])
    for n in range(2):
        tr[2 + n, 0:256, :] = dot(eye, sib_m[n], NT).astype(BF)
        tr[2 + n, 256:320, :] = dot(pick, sib_l[n], NT).astype(BF)
    for m in range(4):
        cols = slice(PAIR * m, PAIR * m + PAIR)
        o = (dot(tr[0], eg[:, cols]) + dot(tr[1], eu[:, cols])
             + dot(tr[2], sib_w[0, :, cols]) + dot(tr[3], sib_w[1, :, cols])).astype(BF)
        fsend[:, cols] = o[0:256]
        lstack[64 * m:64 * m + 64, :] = o[256:320]
    fold = onehot(r == ((k_ >> 2) & 15) * 16 + (k_ >> 6) * 4 + (k_ & 3))
    fsend[:, 3584:BACK] = dot(fold, lstack[...]).astype(BF)
    for k in range(1, 16):
        to = chip(k)
        send(rows16(fsend, to), rows16(frecv, j), f_s.at[k], f_r.at[k], (to * 2 + c, z))
    keep = pltpu.make_async_copy(rows16(fsend, j), rows16(frecv, j), loc.at[2])
    keep.start()
    ring_step(xc_view, xc_half, a_s, a_r, 2)

    def wgrad(out, g0, g1, gl, arr):
        for m in range(4):
            cols = slice(PAIR * m, PAIR * m + PAIR)
            out[:, cols] = (dot(g0, shards[2 * m + arr, 0, :, 0:PAIR])
                            + dot(g1, shards[2 * m + arr, 1, :, 0:PAIR])
                            + dot(gl, lbuf[arr, :, cols])).astype(BF)

    wgrad(out_g, grm[0, 0], grm[1, 0], grl[0], 0)
    ring_step(xc_view, xc_half, a_s, a_r, 3)
    wgrad(out_u, grm[0, 1], grm[1, 1], grl[1], 0)
    wgrad(out_d, hm[0], hm[1], hl[...], 1)

    arrived(group_half(s_over, 0), b_s.at[6], b_r.at[6])
    arrived(group_half(s_over, 1), b_s.at[7], b_r.at[7])
    send(group(s_over), group(s_over), bm_s.at[6], bm_r.at[6], (sib, z))
    ring_end(xc_view, xc_half, a_s, a_r)
    sib_f = c * x + (1 - c) * y
    sib_s = c * y + (1 - c) * x
    o_c = 1 - c
    for n, f in enumerate((0, -1, 1, 2)):
        arrived(wall.at[o_c, sib_s * 4 + shifted(sib_f, f, 4)], bm_s.at[n], bm_r.at[n])
    for n, s in enumerate((-1, 1, 2)):
        arrived(wall.at[o_c, pl.ds(shifted(sib_s, s, 4) * 4, 4)], bm_s.at[4 + n], bm_r.at[4 + n])

    eye128 = onehot(iota((128, 128), 0) == iota((128, 128), 1))

    def dense_forward(n, carry):
        cc, g = lax.div(n, 4), lax.rem(n, 4)
        w = wall[cc, pl.ds(g * 4, 4)].reshape(256, 3584)
        p = dot(w, xc[...], NT)
        gate = p[:, 0:128]
        up = pltpu.roll(gate, 256 - ROWS, 0)
        grad = pltpu.roll(p[:, 128:256], 256 - 2 * ROWS, 0)
        _, gg, gu = swiglu(gate, up, grad)
        row = iota((256, 128), 0) & 63
        shift = pltpu.roll(gu.astype(F32), ROWS, 0)
        both = jnp.where(row < ROWS, gg.astype(F32), jnp.where(row < 2 * ROWS, shift, 0.0)).astype(BF)
        ggt[n] = dot(eye128, both, NT).astype(BF)
        return carry

    lax.fori_loop(0, 8, dense_forward, 0)

    for k in range(1, 16):
        arrived(rows16(frecv, chip_back(k)), f_s.at[k], f_r.at[k])
    keep.wait()
    cq = (iota((128, 256), 1) >> 2) & 3
    cl = comb_l[...]
    for m in range(4):
        cols = slice(PAIR * m, PAIR * m + PAIR)
        total = dot(comb_m[...], frecv[:, cols]) + dot(
            jnp.where(cq == m, cl, jnp.zeros_like(cl)), frecv[:, 3584:BACK])
        for n in range(8):
            cc, g = n // 4, n % 4
            w = wall[cc, 4 * g:4 * g + 4, :, cols].reshape(256, PAIR)
            total = total + dot(ggt[n], w)
        rs_send[2 * m] = total[:, 0:448].astype(BF)
        rs_send[2 * m + 1] = total[:, 448:PAIR].astype(BF)
    for s in range(1, 8):
        to = shifted(z, s, 8)
        send(rs_send.at[to], rs_recv.at[z], r_s.at[s], r_r.at[s], (i, to))
    acc = rs_send[z].astype(F32)
    for s in range(1, 8):
        o = shifted(z, -s, 8)
        arrived(rs_recv.at[o], r_s.at[s], r_r.at[s])
        acc = acc + rs_recv[o].astype(F32)
    out_x[...] = acc.astype(BF)
    for copy in pending:
        copy.wait_send()


def body(
    tokens, cotangent, routes, route_weights, dense_gate, dense_up, dense_down,
    expert_gate, expert_up, expert_down,
):
    z = lax.axis_index("tensor")
    even = z % 2 == 0
    mine = jnp.where(even, tokens, cotangent)
    other = jnp.where(even, cotangent, tokens)
    wblk = jnp.concatenate(
        [dense_gate[0], dense_up[0], dense_down[0], jnp.zeros((64 - 3 * ROWS, 3584), BF)], axis=0)

    ids = routes.reshape(-1)
    n = ids.shape[0]
    order = jnp.arange(n, dtype=jnp.int32)
    ranks = jnp.sum(
        ((ids[:, None] == ids[None, :]) & (order[None, :] < order[:, None])).astype(jnp.int32), axis=1
    ).reshape(routes.shape)
    slot = jnp.arange(256, dtype=jnp.int32)
    main = jnp.where(ranks < 16, routes * 16 + ranks, -1)
    rest = jnp.where(ranks >= 16, routes * 4 + ranks - 16, -1)
    rest_slot = (slot // 16) * 4 + slot % 4
    hit_m = [main[:, t] for t in range(2)]
    hit_l = [rest[:, t] for t in range(2)]
    weights = [jnp.where(even, 1.0, route_weights[:, t]) for t in range(2)]

    def place(hits, slots):
        masks = [h[None, :] == slots[:, None] for h in hits]
        w = sum(jnp.sum(jnp.where(mk, wt[None, :], 0.0), axis=1) for mk, wt in zip(masks, weights))
        return (masks[0] | masks[1]).astype(BF), w[:, None]

    def comb(hits, slots):
        return ((hits[0][:, None] == slots[None, :]) | (hits[1][:, None] == slots[None, :])).astype(BF)

    place_m, w_m = place(hit_m, slot)
    place_l, w_l = place(hit_l, rest_slot)
    comb_m, comb_l = comb(hit_m, slot), comb(hit_l, rest_slot)

    V = pltpu.VMEM
    sem = pltpu.SemaphoreType.DMA
    scratch = [
        V((128, 448), BF),
        V((256, WIDE), BF),
        V((8, 2, 256, WIDE), BF),
        V((2, 128, 3584), BF),
        V((2, 16, 64, 3584), BF),
        V((2, 152, 3584), BF),
        V((2, 2, 152, 256), BF),
        V((2, 152, 128), BF),
        V((2, 152, 256), BF),
        V((152, 128), BF),
        V((2, 152, 256), BF),
        V((2, 152, 128), BF),
        V((4, 320, 152), BF),
        V((256, PAIR), BF),
        V((256, BACK), BF),
        V((256, BACK), BF),
        V((256, 3584), BF),
        V((8, 128, 256), BF),
        V((8, 128, 448), BF),
        V((8, 128, 448), BF),
        sem((2,)), sem((16,)), sem((16,)), sem((8,)), sem((8,)), sem((8,)), sem((8,)),
        sem((8,)), sem((8,)), sem((7,)), sem((7,)), sem((2,)), sem((2,)),
        sem((2,)), sem((2,)), sem((16,)), sem((16,)), sem((8,)), sem((8,)), sem((8,)), sem((8,)),
        sem((3,)),
    ]
    vm = pl.BlockSpec(memory_space=pltpu.VMEM)
    return pl.pallas_call(
        kernel,
        out_shape=(
            jax.ShapeDtypeStruct((128, 448), BF),
            jax.ShapeDtypeStruct((152, 3584), BF),
            jax.ShapeDtypeStruct((152, 3584), BF),
            jax.ShapeDtypeStruct((152, 3584), BF),
        ),
        in_specs=[vm] * 12,
        out_specs=[vm] * 4,
        scratch_shapes=scratch,
        compiler_params=pltpu.CompilerParams(
            collective_id=0, has_side_effects=True, vmem_limit_bytes=62 * 2**20),
    )(mine, other, place_m, place_l, comb_m, comb_l, w_m, w_l, wblk, expert_gate, expert_up, expert_down)


def solution(mesh):
    rows = P(("expert", "tensor"), None)
    dense = P("tensor", "expert", None)
    return jax.shard_map(
        body,
        mesh=mesh,
        in_specs=(
            P("expert", "tensor"), P("expert", "tensor"), P("expert", None), P("expert", None),
            dense, dense, dense, rows, rows, rows,
        ),
        out_specs=(P("expert", "tensor"), rows, rows, rows),
        check_vma=False,
    )
```

time: 776 us -> 167 us (0.22)
  waiting for transfers between devices: 418 us -> 0 us
  local copies, waits for them, and re-layouts: 189 us -> 10.6 us
  Pallas kernels: 0 us -> 149 us
  blocking collectives: 90.5 us -> 0 us
  matrix products: 51.6 us -> 0 us
  between operations: 14.5 us -> 0.76 us
  starting transfers between devices: 8 us -> 0 us
    all_gather x5 -> x0, waiting for transfers between devices: 387 us -> none  [the longest x1 198 us: body(): lax.all_gather(recv_tokens, 'tensor', axis=2, tiled=True)]
    pallas_call x0 -> x1, Pallas kernels: none -> 149 us  [body(): pl.pallas_call(kernel, out_shape=(jax.ShapeDtypeStruct((128, 448), BF), j...]
    unnamed x47 -> x18, local copies, waits for them, and re-layouts: 106 us -> 6.92 us
    all_gather x2 -> x0, blocking collectives: 53.2 us -> none  [the longest x1 26.7 us: body(): lax.all_gather(tokens, 'tensor', axis=1, tiled=True)]
    dot_general x14 -> x0, matrix products: 51.6 us -> none  [the longest x5 18.6 us: dot_rows(): lax.dot_general(left, right, (((1,), (1,)), ((), ())), preferred_element_...]
    all_gather x2 -> x0, local copies, waits for them, and re-layouts: 51.3 us -> none  [the longest x1 25.7 us: body(): lax.all_gather(recv_tokens, 'tensor', axis=2, tiled=True)]
    all_to_all x2 -> x0, blocking collectives: 37.3 us -> none  [the longest x1 19.2 us: body(): lax.all_to_all(send_tokens, 'expert', split_axis=0, concat_axis=0, tiled=...]
    unnamed x9 -> x0, waiting for transfers between devices: 30.8 us -> none
  transfers between devices with their start and end apart: 8 -> 0, of which waited for: 4 -> 0; matrix products, arithmetic and copies ran while one was open for 30% -> 0% of each run, Pallas kernels for 0% -> 0%
where the time goes in v1:
time: 167 us
  Pallas kernels  149 us (89%)
  local copies, waits for them, and re-layouts  10.6 us (6%)
  other arithmetic  6.55 us (4%)
    pallas_call x1, Pallas kernels, body(): pl.pallas_call(kernel, out_shape=(jax.ShapeDtypeStruct((128, 448), BF), j...  149 us
    unnamed x18, local copies, waits for them, and re-layouts  6.92 us

profile of v1, /device:TPU:16, one launch (start us, length us, event | category | flops | bytes accessed | tf_op | source)
XLA Modules:
  0.0 166.6 jit_solution(9929014353108402715)
XLA Ops:
  0.7 0.1 pad.3.clone
  0.8 0.9 fusion.10
  1.6 0.8 copy.59
  2.4 0.1 eq.135
  2.6 0.2 convert_reduce_fusion
  2.7 0.1 reshape.101
  3.0 0.7 compare_select_fusion.2
  3.7 0.3 fusion.2
  4.0 0.7 or_convert_fusion.comb_l
  4.7 0.7 fusion.5.place_l
  5.4 0.7 fusion.7.comb_m
  6.2 0.7 fusion.4.place_m
  6.8 0.8 copy.64.w_m
  7.6 0.8 copy.65.w_l
  8.4 1.0 copy.55
  9.4 0.1 copy.56
  9.6 0.7 broadcast_select_fusion
  10.3 0.9 maximum_maximum_fusion.wblk
  11.2 148.6 %shard_map.129 = (bf16[128,448]{1,0:T(8,128)(2,1)}, bf16[152,3584]{1,0:T(8,128)(2,1)}, bf16[152,3584]{1,0:T(8,128)(2,1)}, bf16[152,3584]{1,0:T(8,128)(2,1)}) custom-call(bf16[128,448]{1,0:T(8,128)(2,1)} %get-tuple-element.29.mine, bf16[128,448]{1,0:T(8,128)(2,1)} %get-tuple-element.28.other, bf16[256,128]{1,0:T(8,128)(2,1)} %fusion.4.place_m, ...), custom_call_target="tpu_custom_call" | custom-call | tf_op jit(solution)/shard_map/pallas_call | solution.py:439
  159.9 1.7 %copy.66 = bf16[128,448]{0,1:T(8,128)(2,1)} copy(bf16[128,448]{1,0:T(8,128)(2,1)} %get-tuple-element.20) | data formatting | bytes 229376 | tf_op jit(solution)/shard_map/pallas_call | solution.py:439
  161.6 2.4 %copy.70 = bf16[152,3584]{1,0:T(8,128)(2,1)} copy(bf16[152,3584]{1,0:T(8,128)(2,1)} %get-tuple-element.45) | data formatting | bytes 2179072
  163.9 1.0 copy.71
  164.9 0.6 copy-done
  165.6 1.0 copy.72
  (17 shorter events, 0.1 us)
Async XLA Ops:
  0.6 9.7 %copy-start.2 = (bf16[1,19,3584]{2,1,0:T(8,128)(2,1)S(1)}, bf16[1,19,3584]{2,1,0:T(8,128)(2,1)}, u32[]{:S(2)}) copy-start(bf16[1,19,3584]{2,1,0:T(8,128)(2,1)} %param.16) | copy-start | bytes 408580
  0.6 9.7 %copy-start.3 = (bf16[1,19,3584]{2,1,0:T(8,128)(2,1)S(1)}, bf16[1,19,3584]{2,1,0:T(8,128)(2,1)}, u32[]{:S(2)}) copy-start(bf16[1,19,3584]{2,1,0:T(8,128)(2,1)} %param.15) | copy-start | bytes 408580
  0.7 9.6 %copy-start.4 = (bf16[1,19,3584]{2,1,0:T(8,128)(2,1)S(1)}, bf16[1,19,3584]{2,1,0:T(8,128)(2,1)}, u32[]{:S(2)}) copy-start(bf16[1,19,3584]{2,1,0:T(8,128)(2,1)} %param.14) | copy-start | bytes 408580
  0.7 8.8 %copy-start.5 = (bf16[128,448]{0,1:T(8,128)(2,1)S(1)}, bf16[128,448]{0,1:T(8,128)(2,1)}, u32[]{:S(2)}) copy-start(bf16[128,448]{0,1:T(8,128)(2,1)} %param.11) | copy-start | bytes 344068
  161.6 2.4 %copy-start.1 = (bf16[152,3584]{1,0:T(8,128)(2,1)S(1)}, bf16[152,3584]{1,0:T(8,128)(2,1)}, u32[]{:S(2)}) copy-start(bf16[152,3584]{1,0:T(8,128)(2,1)} %get-tuple-element.46) | copy-start | bytes 3268612
  163.9 1.6 copy-start

commit v2 on v0

v2 whole, which is shorter than its diff:
```python
import jax
import jax.numpy as jnp
from jax import lax
from jax.experimental import pallas as pl
from jax.experimental.pallas import tpu as pltpu
from jax.sharding import PartitionSpec as P

MESH = pl.DeviceIdType.MESH
BF, F32 = jnp.bfloat16, jnp.float32
NT = (((1,), (1,)), ((), ()))
NN = (((1,), (0,)), ((), ()))
ROWS = 19
PAIR = 896
WIDE = 1152


def dot(a, b, dims=NN):
    return lax.dot_general(a, b, dims, preferred_element_type=F32)


def iota(shape, dim):
    return lax.broadcasted_iota(jnp.int32, shape, dim)


def onehot(mask):
    return jnp.where(mask, 1.0, 0.0).astype(BF)


def swiglu(gate, up, grad):
    sig = 1.0 / (1.0 + jnp.exp(-gate))
    silu = gate * sig
    slope = sig * (1.0 + gate * (1.0 - sig))
    return silu, (grad * up * slope).astype(BF), (grad * silu).astype(BF)


def route_masks(routes, weights, even, place_m, place_l, comb_m, comb_l, w_m, w_l):
    t0, t1 = iota((128, 128), 0), iota((128, 128), 1)
    eye = t0 == t1
    ids = routes[...].astype(F32)
    row = [ids[k:k + 1, :] for k in range(2)]
    col = [jnp.sum(jnp.where(eye, r, 0.0), axis=1, keepdims=True) for r in row]

    def count(same, ahead, axis):
        n = sum(jnp.where(s & ahead, 1.0, 0.0) for s in same)
        return jnp.sum(n, axis=axis, keepdims=True)

    row_rank = [count([c == r for c in col], t0 < t1, 0) for r in row]
    col_rank = [count([r == c for r in row], t1 < t0, 1) for c in col]

    def slots(ids, ranks):
        main = [jnp.where(k < 16, e * 16 + k, -1.0) for e, k in zip(ids, ranks)]
        rest = [jnp.where(k >= 16, e * 4 + k - 16, -1.0) for e, k in zip(ids, ranks)]
        return main, rest

    def fill(place, w, hits, slot):
        masks = [h == slot for h in hits]
        place[...] = onehot(masks[0] | masks[1])
        picked = sum(jnp.where(mk, weights[k:k + 1, :], 0.0) for k, mk in enumerate(masks))
        picked = jnp.sum(picked, axis=1, keepdims=True)
        w[...] = jnp.where(even, jnp.ones_like(picked), picked)

    main, rest = slots(row, row_rank)
    s = iota((256, 128), 0)
    fill(place_m, w_m, main, s.astype(F32))
    fill(place_l, w_l, rest, ((s >> 4) * 4 + (s & 3)).astype(F32))
    main, rest = slots(col, col_rank)
    s = iota((128, 256), 1)
    sf, sl = s.astype(F32), ((s >> 4) * 4 + (s & 3)).astype(F32)
    comb_m[...] = onehot((main[0] == sf) | (main[1] == sf))
    comb_l[...] = onehot((rest[0] == sl) | (rest[1] == sl))


def kernel(
    tok_in, cot_in, routes_in, weights_in, dg_in, du_in, dd_in, eg_in, eu_in, ed_in,
    out_x, out_g, out_u, out_d,
    tok, cot, routes, weights, dg, du, dd, eg, eu, ed, res, place_m, place_l, comb_m, comb_l, w_m, w_l, unfold, fold, wblk, oth, blk,
    packed, shards, lbuf, wall, sib_w, acc, accl, grm, grl, hm, hl, sib_m, sib_l,
    tr, fsend, frecv, xc, ggt, dense, rs_send, rs_recv,
    p_s, p_r, c_s, c_r, d_s, d_r, m_s, m_r, b_s, b_r, bm_s, bm_r, w_s, w_r,
    g_s, g_r, f_s, f_r, a_s, a_r, r_s, r_r, loc,
):
    i = lax.axis_index("expert")
    z = lax.axis_index("tensor")
    c = lax.rem(i, 2)
    j = lax.div(i, 2)
    y, x = lax.div(j, 4), lax.rem(j, 4)
    sib = i + 1 - 2 * c
    par = lax.rem(z, 2)
    even = par == 0
    first = (1 - c) * x + c * y
    second = (1 - c) * y + c * x

    def plane(f, s):
        yy = (1 - c) * s + c * f
        xx = (1 - c) * f + c * s
        return ((yy * 4 + xx) * 2 + c, z)

    def shifted(v, s, n):
        return lax.rem(v + s + n, n)

    pending = []

    def send(src, dst, s_sem, r_sem, n, dev):
        copy = pltpu.make_async_remote_copy(
            src_ref=src, dst_ref=dst, send_sem=s_sem.at[n], recv_sem=r_sem.at[n],
            device_id=dev, device_id_type=MESH,
        )
        copy.start()
        pending.append(copy)

    def arrived(ref, s_sem, r_sem, n):
        pltpu.make_async_remote_copy(
            src_ref=ref, dst_ref=ref, send_sem=s_sem.at[0], recv_sem=r_sem.at[n],
            device_id=(sib, z), device_id_type=MESH,
        ).wait_recv()

    def local(src, dst, n):
        copy = pltpu.make_async_copy(src, dst, loc.at[n])
        copy.start()
        return copy

    offsets = ((0, 0), (1, 0), (0, 1), (3, 0), (0, 3), (1, 1), (3, 3), (2, 0), (0, 2), (1, 3), (3, 1),
               (2, 1), (1, 2), (2, 3), (3, 2), (2, 2))

    def chip(k, sign=1):
        p, q = ((sign * v) % 4 for v in offsets[k])
        return (lax.rem(y + (1 - c) * q + c * p, 4) * 4 + lax.rem(x + (1 - c) * p + c * q, 4))

    def chip_back(k):
        return chip(k, -1)

    barrier = pltpu.get_barrier_semaphore()
    for k in range(1, 16):
        pl.semaphore_signal(barrier, inc=1, device_id=(chip(k) * 2 + c, z), device_id_type=MESH)
    pl.semaphore_signal(barrier, inc=1, device_id=(sib, z), device_id_type=MESH)
    for s in range(1, 8):
        pl.semaphore_signal(barrier, inc=1, device_id=(i, shifted(z, s, 8)), device_id_type=MESH)
    early = [local(src, dst, 12 + n) for n, (src, dst) in enumerate((
        (tok_in, tok), (cot_in, cot), (dg_in, dg), (du_in, du), (dd_in, dd),
        (routes_in, routes), (weights_in, weights)))]
    loads = [local(eg_in, eg, 0), local(eu_in, eu, 1), local(ed_in, ed, 2)]
    for copy in early:
        copy.wait()

    t, ct = tok[...], cot[...]
    half = pl.ds(pl.multiple_of(448 * par, 64), 448)
    oth[...] = jnp.where(even, ct, t)
    blk[half, :] = jnp.where(even, t, ct)
    at, k_ = iota((64, ROWS), 0), iota((64, ROWS), 1)
    wblk[...] = sum(
        dot(onehot(at == k_ + ROWS * n), m[0]) for n, m in enumerate((dg, du, dd))).astype(BF)
    pl.semaphore_wait(barrier, 23)

    partner = z + 1 - 2 * par
    send(oth, blk.at[half, :], p_s, p_r, 0, (i, partner))

    def block(pos, h):
        return wall.at[c, pos, pl.ds(32 * h, 32), :]

    own_pos = second * 4 + first
    here = local(wblk, wall.at[c, own_pos], 3)
    send(wblk, wall.at[c, own_pos], b_s, b_r, 0, plane(shifted(first, 1, 4), second))
    send(wblk, wall.at[c, own_pos], b_s, b_r, 1, plane(shifted(first, -1, 4), second))

    route_masks(routes, weights, even, place_m, place_l, comb_m, comb_l, w_m, w_l)
    r, k_ = iota((256, 256), 0), iota((256, 256), 1)
    unfold[...] = onehot(k_ == ((r >> 2) & 15) * 16 + (r >> 6) * 4 + (r & 3))
    fold[...] = onehot(r == ((k_ >> 2) & 15) * 16 + (k_ >> 6) * 4 + (k_ & 3))
    acc[...] = jnp.zeros_like(acc)
    accl[...] = jnp.zeros_like(accl)

    right, left_z = shifted(z, 1, 8), shifted(z, -1, 8)

    def ring_start(view, s_sem, r_sem):
        send(view(z), view(z), s_sem, r_sem, 0, (i, right))
        send(view(z), view(z), s_sem, r_sem, 4, (i, left_z))

    def ring_step(view, half, s_sem, r_sem, s):
        o = shifted(z, -s, 8)
        arrived(view(o), s_sem, r_sem, s - 1)
        part = view(o) if s < 3 else half(o, 0)
        send(part, part, s_sem, r_sem, s, (i, right))
        o = shifted(z, s, 8)
        arrived(view(o), s_sem, r_sem, s + 3)
        part = view(o) if s < 3 else half(o, 1)
        send(part, part, s_sem, r_sem, s + 4, (i, left_z))

    def ring_end(half, s_sem, r_sem):
        o = shifted(z, 4, 8)
        arrived(half(o, 0), s_sem, r_sem, 3)
        arrived(half(o, 1), s_sem, r_sem, 7)

    def xc_cols(o):
        return pl.ds(pl.multiple_of(lax.div(o, 2) * PAIR, 128), PAIR)

    def xc_view(o):
        return xc.at[pl.ds(pl.multiple_of(lax.rem(o, 2) * 128, 128), 128), xc_cols(o)]

    def xc_half(o, h):
        return xc.at[pl.ds(pl.multiple_of(lax.rem(o, 2) * 128 + 64 * h, 64), 64), xc_cols(o)]

    eye128 = onehot(iota((128, 128), 0) == iota((128, 128), 1))
    arrived(blk.at[pl.ds(pl.multiple_of(448 * (1 - par), 64), 448), :], p_s, p_r, 0)
    xc[pl.ds(pl.multiple_of(par * 128, 128), 128), xc_cols(z)] = dot(eye128, blk[...], NT).astype(BF)
    ring_start(xc_view, a_s, a_r)

    packed[:, 0:PAIR] = (dot(place_m[...], blk[...], NT) * w_m[...]).astype(BF)
    quarter = (iota((256, 128), 0) >> 2) & 3
    sel = [jnp.where(quarter == q, place_l[...], jnp.zeros((256, 128), BF)) for q in range(4)]
    left = [sum(dot(sel[q], blk[256 * q + 128 * h:256 * q + 128 * h + 128, :], NT)
                for q in range(4) if 256 * q + 128 * h < PAIR) for h in range(2)]
    for h in range(2):
        packed[:, PAIR + 128 * h:PAIR + 128 * h + 128] = (left[h] * w_l[...]).astype(BF)

    def rows16(ref, n):
        return ref.at[pl.ds(pl.multiple_of(16 * n, 16), 16), :]

    own_shard = shards.at[z, c]
    for k in range(1, 16):
        to = chip(k)
        send(rows16(packed, to), rows16(own_shard, j), c_s, c_r, k, (to * 2 + c, z))
    keep = local(rows16(packed, j), rows16(own_shard, j), 4)
    here.wait()
    send(wall.at[c, own_pos], wall.at[c, own_pos], bm_s, bm_r, 0, (sib, z))
    for copy in loads:
        copy.wait()
    send(eg, sib_w.at[0], w_s, w_r, 0, (sib, z))
    send(eu, sib_w.at[1], w_s, w_r, 1, (sib, z))

    before = second * 4 + shifted(first, -1, 4)
    after = second * 4 + shifted(first, 1, 4)
    across = second * 4 + shifted(first, 2, 4)
    arrived(wall.at[c, before], b_s, b_r, 0)
    send(block(before, 0), block(before, 0), b_s, b_r, 2, plane(shifted(first, 1, 4), second))
    arrived(wall.at[c, after], b_s, b_r, 1)
    send(block(after, 1), block(after, 1), b_s, b_r, 3, plane(shifted(first, -1, 4), second))
    ring_step(xc_view, xc_half, a_s, a_r, 1)
    for k in range(1, 16):
        arrived(rows16(own_shard, chip_back(k)), c_s, c_r, k)
    keep.wait()

    def shard_half(o, h):
        return shards.at[o, c, pl.ds(128 * h, 128), :]

    def mirror(s):
        o = shifted(z, s, 8)
        send(shards.at[o, c], shards.at[o, c], m_s, m_r, s, (sib, z))

    def group(g):
        return wall.at[c, pl.ds(g * 4, 4)]

    def group_half(g, h):
        return wall.at[c, pl.ds(g * 4 + 2 * h, 2)]

    def right_hop(s, h):
        o = shifted(z, -s, 8)
        if s:
            arrived(shard_half(o, h), d_s, d_r, 2 * s - 2 + h)
        if s < 3 or h == 0:
            send(shard_half(o, h), shard_half(o, h), d_s, d_r, 2 * s + h, (i, right))

    def left_hop(s, h):
        o = shifted(z, s, 8)
        if s:
            arrived(shard_half(o, h), d_s, d_r, 8 + 2 * s - 2 + h)
        if s < 3 or h == 1:
            send(shard_half(o, h), shard_half(o, h), d_s, d_r, 8 + 2 * s + h, (i, left_z))

    def hop(s, part):
        right_hop(s, part)
        left_hop(s, 1 - part)

    hop(0, 0)
    hop(0, 1)
    arrived(block(across, 0), b_s, b_r, 2)
    arrived(block(across, 1), b_s, b_r, 3)
    s_up, s_down, s_over = (shifted(second, 1, 4), shifted(second, -1, 4), shifted(second, 2, 4))
    send(group(second), group(second), b_s, b_r, 4, plane(first, s_up))
    send(group(second), group(second), b_s, b_r, 5, plane(first, s_down))
    mirror(0)
    send(wall.at[c, before], wall.at[c, before], bm_s, bm_r, 1, (sib, z))
    send(wall.at[c, after], wall.at[c, after], bm_s, bm_r, 2, (sib, z))
    send(wall.at[c, across], wall.at[c, across], bm_s, bm_r, 3, (sib, z))

    def absorb(s):
        o = shifted(z, s, 8)
        arrived(shards.at[o, 1 - c], m_s, m_r, s)
        base = lax.div(o, 2) * PAIR
        cols = pl.ds(pl.multiple_of(base, 128), PAIR)
        arr = lax.rem(o, 2)
        for cc in range(2):
            flat = dot(unfold[...], shards[o, cc, :, PAIR:WIDE]).astype(BF)
            for q in range(4):
                n = 256 if q < 3 else 128
                lbuf[arr, 64 * cc:64 * cc + 64, pl.ds(pl.multiple_of(base + 256 * q, 128), n)] = (
                    flat[64 * q:64 * q + 64, 0:n])

        def add(n, w):
            wc = w[:, cols]
            for cc in range(2):
                acc[n, cc] += dot(wc, shards[o, cc, :, 0:PAIR], NT)
            accl[n] += dot(wc, lbuf[arr, :, cols], NT)

        @pl.when(arr == 0)
        def _():
            add(0, eg)
            add(1, eu)

        @pl.when(arr == 1)
        def _():
            add(2, ed)

    o_c = 1 - c
    sib_f = c * x + (1 - c) * y
    sib_s = c * y + (1 - c) * x

    def dense_forward(cc, g):
        w = wall[cc, pl.ds(g * 4, 4)].reshape(256, 3584)
        p = dot(w, xc[...], NT)
        gate = p[:, 0:128]
        up = pltpu.roll(gate, 256 - ROWS, 0)
        grad = pltpu.roll(p[:, 128:256], 256 - 2 * ROWS, 0)
        _, gg, gu = swiglu(gate, up, grad)
        row = iota((256, 128), 0) & 63
        shift = pltpu.roll(gu.astype(F32), ROWS, 0)
        both = jnp.where(row < ROWS, gg.astype(F32), jnp.where(row < 2 * ROWS, shift, 0.0)).astype(BF)
        ggt[cc * 4 + g] = dot(eye128, both, NT).astype(BF)

    def dense_back(n, carry):
        cols = pl.ds(pl.multiple_of(n * 512, 128), 512)
        dense[:, cols] = sum(
            dot(ggt[k], wall[k // 4, 4 * (k % 4):4 * (k % 4) + 4, :, cols].reshape(256, 512))
            for k in range(8))
        return carry

    ring_step(xc_view, xc_half, a_s, a_r, 2)
    absorb(0)
    hop(1, 0)
    ring_step(xc_view, xc_half, a_s, a_r, 3)
    hop(1, 1)
    mirror(1)
    mirror(7)
    absorb(1)
    absorb(7)
    hop(2, 0)
    arrived(group(s_down), b_s, b_r, 4)
    send(group_half(s_down, 0), group_half(s_down, 0), b_s, b_r, 6, plane(first, s_up))
    send(group(s_down), group(s_down), bm_s, bm_r, 4, (sib, z))
    arrived(group(s_up), b_s, b_r, 5)
    send(group_half(s_up, 1), group_half(s_up, 1), b_s, b_r, 7, plane(first, s_down))
    send(group(s_up), group(s_up), bm_s, bm_r, 5, (sib, z))
    hop(2, 1)
    mirror(2)
    mirror(6)
    ring_end(xc_half, a_s, a_r)
    for n, f in enumerate((0, -1, 1, 2)):
        arrived(wall.at[o_c, sib_s * 4 + shifted(sib_f, f, 4)], bm_s, bm_r, n)
    dense_forward(c, second)
    dense_forward(o_c, sib_s)
    absorb(2)
    absorb(6)
    hop(3, 0)
    arrived(group_half(s_over, 0), b_s, b_r, 6)
    arrived(group_half(s_over, 1), b_s, b_r, 7)
    send(group(s_over), group(s_over), bm_s, bm_r, 6, (sib, z))
    dense_forward(c, s_down)
    dense_forward(c, s_up)
    for n, s in enumerate((-1, 1)):
        g = shifted(sib_s, s, 4)
        arrived(wall.at[o_c, pl.ds(g * 4, 4)], bm_s, bm_r, 4 + n)
        dense_forward(o_c, g)
    hop(3, 1)
    mirror(3)
    mirror(5)
    absorb(3)
    absorb(5)
    arrived(shard_half(shifted(z, 4, 8), 0), d_s, d_r, 6)
    arrived(shard_half(shifted(z, 4, 8), 1), d_s, d_r, 15)
    mirror(4)
    absorb(4)

    for cc in range(2):
        silu, gg, gu = swiglu(acc[0, cc], acc[1, cc], acc[2, cc])
        hm[cc] = (silu * acc[1, cc]).astype(BF)
        grm[cc, 0] = gg
        grm[cc, 1] = gu
    silu, gg, gu = swiglu(accl[0], accl[1], accl[2])
    hl[...] = (silu * accl[1]).astype(BF)
    grl[0] = gg
    grl[1] = gu
    send(grm.at[1 - c], sib_m, g_s, g_r, 0, (sib, z))
    send(grl, sib_l, g_s, g_r, 1, (sib, z))

    eye = onehot(iota((256, 256), 0) == iota((256, 256), 1))
    pick = onehot(iota((64, 128), 1) == iota((64, 128), 0) + 64 * c)
    arrived(sib_w.at[0], w_s, w_r, 0)
    arrived(sib_w.at[1], w_s, w_r, 1)
    for n in range(2):
        tr[n, 0:256, :] = dot(eye, grm[c, n], NT).astype(BF)
        tr[n, 256:320, :] = dot(pick, grl[n], NT).astype(BF)
    arrived(sib_m, g_s, g_r, 0)
    arrived(sib_l, g_s, g_r, 1)
    for n in range(2):
        tr[2 + n, 0:256, :] = dot(eye, sib_m[n], NT).astype(BF)
        tr[2 + n, 256:320, :] = dot(pick, sib_l[n], NT).astype(BF)

    pair = lax.div(z, 2)
    chunk = [shifted(pair, 1 + k, 4) for k in range(4)]
    keeps = []
    for k in range(4):
        cols = pl.ds(pl.multiple_of(chunk[k] * PAIR, 128), PAIR)
        o = (dot(tr[0], eg[:, cols]) + dot(tr[1], eu[:, cols])
             + dot(tr[2], sib_w[0, :, cols]) + dot(tr[3], sib_w[1, :, cols])).astype(BF)
        fsend[k, :, 0:PAIR] = o[0:256]
        tail = o[256:320]
        stack = jnp.concatenate(
            [tail[:, 0:256], tail[:, 256:512], tail[:, 512:768],
             jnp.concatenate([tail[:, 768:896], jnp.zeros((64, 128), BF)], axis=1)], axis=0)
        fsend[k, :, PAIR:WIDE] = dot(fold[...], stack).astype(BF)
        for n in range(1, 16):
            to = chip(n)
            send(rows16(fsend.at[k], to), rows16(frecv.at[k], j), f_s, f_r, 16 * k + n, (to * 2 + c, z))
        keeps.append(local(rows16(fsend.at[k], j), rows16(frecv.at[k], j), 5 + k))

    outs = []

    def wgrad(n, out, g0, g1, gl, arr):
        def cols_of(m, carry):
            cols = pl.ds(pl.multiple_of(m * PAIR, 128), PAIR)
            res[n, :, cols] = (dot(g0, shards[2 * m + arr, 0, :, 0:PAIR])
                               + dot(g1, shards[2 * m + arr, 1, :, 0:PAIR])
                               + dot(gl, lbuf[arr, :, cols])).astype(BF)
            return carry

        lax.fori_loop(0, 4, cols_of, 0)
        outs.append(local(res.at[n], out, 9 + n))

    cq = (iota((128, 256), 1) >> 2) & 3

    def combine(k):
        for n in range(1, 16):
            arrived(rows16(frecv.at[k], chip_back(n)), f_s, f_r, 16 * k + n)
        keeps[k].wait()
        m = chunk[k]
        total = dense[:, pl.ds(pl.multiple_of(m * PAIR, 128), PAIR)] + dot(comb_m[...], frecv[k, :, 0:PAIR])
        parts = []
        for q in range(4):
            n = 256 if q < 3 else 128
            sel = jnp.where(cq == q, comb_l[...], jnp.zeros((128, 256), BF))
            parts.append(dot(sel, frecv[k, :, PAIR:PAIR + n]))
        total = total + jnp.concatenate(parts, axis=1)
        flip = total.T.astype(BF)
        for h in range(2):
            rs_send[2 * m + h] = flip[448 * h:448 * h + 448]
        if k < 3:
            for h in range(2):
                to = 2 * m + h
                copy = pltpu.make_async_remote_copy(
                    src_ref=rs_send.at[to], dst_ref=rs_recv.at[z], send_sem=r_s.at[2 * k + h],
                    recv_sem=r_r.at[2 * k + par], device_id=(i, to), device_id_type=MESH)
                copy.start()
                pending.append(copy)
        else:
            send(rs_send.at[partner], rs_recv.at[z], r_s, r_r, 6, (i, partner))

    dense_forward(c, s_over)
    g = shifted(sib_s, 2, 4)
    arrived(wall.at[o_c, pl.ds(g * 4, 4)], bm_s, bm_r, 6)
    dense_forward(o_c, g)
    lax.fori_loop(0, 7, dense_back, 0)
    wgrad(0, out_g, grm[0, 0], grm[1, 0], grl[0], 0)
    combine(0)
    wgrad(1, out_u, grm[0, 1], grm[1, 1], grl[1], 0)
    combine(1)
    wgrad(2, out_d, hm[0], hm[1], hl[...], 1)
    combine(2)
    combine(3)
    total = rs_send[z].astype(F32)
    for k in range(3):
        for h in range(2):
            o = 2 * shifted(pair, -1 - k, 4) + h
            arrived(rs_recv.at[o], r_s, r_r, 2 * k + h)
            total = total + rs_recv[o].astype(F32)
    arrived(rs_recv.at[partner], r_s, r_r, 6)
    out_x[...] = (total + rs_recv[partner].astype(F32)).astype(BF)
    for copy in pending:
        copy.wait_send()
    for copy in outs:
        copy.wait()


def copy_out(a, b, c, d, oa, ob, oc, od, va, vb, vc, vd, sems):
    arrays = ((a, va, oa), (b, vb, ob), (c, vc, oc), (d, vd, od))
    loads = [pltpu.make_async_copy(s, v, sems.at[n]) for n, (s, v, _) in enumerate(arrays)]
    stores = [pltpu.make_async_copy(v, t, sems.at[4 + n]) for n, (_, v, t) in enumerate(arrays)]
    for copy in loads:
        copy.start()
    for load, store in zip(loads, stores):
        load.wait()
        store.start()
    for store in stores:
        store.wait()


def body(
    tokens, cotangent, routes, route_weights, dense_gate, dense_up, dense_down,
    expert_gate, expert_up, expert_down,
):
    V = pltpu.VMEM
    scratch = [
        V((448, 128), BF), V((448, 128), BF),
        V((2, 128), jnp.int32), V((2, 128), F32),
        V((1, ROWS, 3584), BF), V((1, ROWS, 3584), BF), V((1, ROWS, 3584), BF),
        V((152, 3584), BF), V((152, 3584), BF), V((152, 3584), BF),
        V((3, 152, 3584), BF),
        V((256, 128), BF), V((256, 128), BF),
        V((128, 256), BF), V((128, 256), BF),
        V((256, 1), F32), V((256, 1), F32),
        V((256, 256), BF), V((256, 256), BF),
        V((64, 3584), BF),
        V((448, 128), BF),
        V((896, 128), BF),
        V((256, WIDE), BF),
        V((8, 2, 256, WIDE), BF),
        V((2, 128, 3584), BF),
        V((2, 16, 64, 3584), BF),
        V((2, 152, 3584), BF),
        V((3, 2, 152, 256), F32),
        V((3, 152, 128), F32),
        V((2, 2, 152, 256), BF),
        V((2, 152, 128), BF),
        V((2, 152, 256), BF),
        V((152, 128), BF),
        V((2, 152, 256), BF),
        V((2, 152, 128), BF),
        V((4, 320, 152), BF),
        V((4, 256, WIDE), BF),
        V((4, 256, WIDE), BF),
        V((256, 3584), BF),
        V((8, 128, 256), BF),
        V((128, 3584), F32),
        V((8, 448, 128), BF),
        V((8, 448, 128), BF),
    ]
    for n in (1, 16, 16, 8, 8, 7, 2, 2, 64, 8, 7):
        scratch += [pltpu.SemaphoreType.DMA((n,))] * 2
    scratch.append(pltpu.SemaphoreType.DMA((19,)))
    vm = pl.BlockSpec(memory_space=pltpu.VMEM)
    hbm = pl.BlockSpec(memory_space=pl.ANY)
    shapes = (jax.ShapeDtypeStruct((448, 128), BF),) + (jax.ShapeDtypeStruct((152, 3584), BF),) * 3
    results = pl.pallas_call(
        kernel,
        out_shape=shapes,
        in_specs=[hbm] * 10,
        out_specs=[vm] + [hbm] * 3,
        scratch_shapes=scratch,
        compiler_params=pltpu.CompilerParams(
            collective_id=0, has_side_effects=True, vmem_limit_bytes=62 * 2**20),
    )(tokens.T, cotangent.T, routes.T, route_weights.T, dense_gate, dense_up, dense_down,
      expert_gate, expert_up, expert_down)
    x, g, u, d = pl.pallas_call(
        copy_out,
        out_shape=shapes,
        in_specs=[hbm] * 4,
        out_specs=[hbm] * 4,
        scratch_shapes=[V(s.shape, BF) for s in shapes] + [pltpu.SemaphoreType.DMA((8,))],
        compiler_params=pltpu.CompilerParams(vmem_limit_bytes=62 * 2**20),
    )(*results)
    return x.T, g, u, d


def solution(mesh):
    rows = P(("expert", "tensor"), None)
    dense = P("tensor", "expert", None)
    return jax.shard_map(
        body,
        mesh=mesh,
        in_specs=(
            P("expert", "tensor"), P("expert", "tensor"), P("expert", None), P("expert", None),
            dense, dense, dense, rows, rows, rows,
        ),
        out_specs=(P("expert", "tensor"), rows, rows, rows),
        check_vma=False,
    )
```

time: 776 us -> 130 us (0.17)
  waiting for transfers between devices: 418 us -> 0 us
  local copies, waits for them, and re-layouts: 189 us -> 0 us
  Pallas kernels: 0 us -> 127 us
  blocking collectives: 90.5 us -> 0 us
  matrix products: 51.6 us -> 0 us
  between operations: 14.5 us -> 0.8 us
  starting transfers between devices: 8 us -> 0 us
    all_gather x5 -> x0, waiting for transfers between devices: 387 us -> none  [the longest x1 198 us: body(): lax.all_gather(recv_tokens, 'tensor', axis=2, tiled=True)]
    pallas_call x0 -> x2, Pallas kernels: none -> 127 us  [the longest x1 124 us: body(): pl.pallas_call(kernel, out_shape=shapes, in_specs=[hbm] * 10, out_specs=[...]
    unnamed x47 -> x0, local copies, waits for them, and re-layouts: 106 us -> none
    all_gather x2 -> x0, blocking collectives: 53.2 us -> none  [the longest x1 26.7 us: body(): lax.all_gather(tokens, 'tensor', axis=1, tiled=True)]
    dot_general x14 -> x0, matrix products: 51.6 us -> none  [the longest x5 18.6 us: dot_rows(): lax.dot_general(left, right, (((1,), (1,)), ((), ())), preferred_element_...]
    all_gather x2 -> x0, local copies, waits for them, and re-layouts: 51.3 us -> none  [the longest x1 25.7 us: body(): lax.all_gather(recv_tokens, 'tensor', axis=2, tiled=True)]
    all_to_all x2 -> x0, blocking collectives: 37.3 us -> none  [the longest x1 19.2 us: body(): lax.all_to_all(send_tokens, 'expert', split_axis=0, concat_axis=0, tiled=...]
    unnamed x9 -> x0, waiting for transfers between devices: 30.8 us -> none
  transfers between devices with their start and end apart: 8 -> 0, of which waited for: 4 -> 0; matrix products, arithmetic and copies ran while one was open for 30% -> 0% of each run, Pallas kernels for 0% -> 0%
where the time goes in v2:
time: 130 us; the launch traced here: 127 us
  Pallas kernels  127 us (98%)
    pallas_call x1, Pallas kernels, body(): pl.pallas_call(kernel, out_shape=shapes, in_specs=[hbm] * 10, out_specs=[...  124 us
    pallas_call x1, Pallas kernels, body(): pl.pallas_call(copy_out, out_shape=shapes, in_specs=[hbm] * 4, out_specs=...  3.08 us

profile of v2, /device:TPU:16, one launch (start us, length us, event | category | flops | bytes accessed | tf_op | source)
XLA Modules:
  0.0 127.4 jit_solution(17285542816243416627)
XLA Ops:
  0.6 123.5 %shard_map.129 = (bf16[448,128]{1,0:T(8,128)(2,1)}, bf16[152,3584]{1,0:T(8,128)(2,1)}, bf16[152,3584]{1,0:T(8,128)(2,1)}, bf16[152,3584]{1,0:T(8,128)(2,1)}) custom-call(bf16[448,128]{1,0:T(8,128)(2,1)} %bitcast.5, bf16[448,128]{1,0:T(8,128)(2,1)} %bitcast.6, s32[2,128]{1,0:T(2,128)} %bitcast.7, f32[2,128]{1,0:T(2,128)} %bitcast.8, ...), custom_call_target="tpu_custom_call" | custom-call | tf_op jit(solution)/shard_map/pallas_call | solution.py:551
  124.2 3.1 %shard_map.130 = (bf16[448,128]{1,0:T(8,128)(2,1)}, bf16[152,3584]{1,0:T(8,128)(2,1)}, bf16[152,3584]{1,0:T(8,128)(2,1)}, bf16[152,3584]{1,0:T(8,128)(2,1)}) custom-call(bf16[448,128]{1,0:T(8,128)(2,1)} %get-tuple-element.12.a, bf16[152,3584]{1,0:T(8,128)(2,1)} %get-tuple-element.13.b, bf16[152,3584]{1,0:T(8,128)(2,1)} %get-tuple-element.14.c, ...), custom_call_target="tpu_custom_call" | custom-call | tf_op jit(solution)/shard_map/pallas_call | solution.py:561

commit v3 on v2

v3 whole, which is shorter than its diff:
```python
import jax
import jax.numpy as jnp
from jax import lax
from jax.experimental import pallas as pl
from jax.experimental.pallas import tpu as pltpu
from jax.sharding import PartitionSpec as P

MESH = pl.DeviceIdType.MESH
BF, F32 = jnp.bfloat16, jnp.float32
NT = (((1,), (1,)), ((), ()))
NN = (((1,), (0,)), ((), ()))
ROWS = 19
PAIR = 896
WIDE = 1152


def dot(a, b, dims=NN):
    return lax.dot_general(a, b, dims, preferred_element_type=F32)


def iota(shape, dim):
    return lax.broadcasted_iota(jnp.int32, shape, dim)


def onehot(mask):
    return jnp.where(mask, 1.0, 0.0).astype(BF)


def swiglu(gate, up, grad):
    sig = 1.0 / (1.0 + jnp.exp(-gate))
    silu = gate * sig
    slope = sig * (1.0 + gate * (1.0 - sig))
    return silu, (grad * up * slope).astype(BF), (grad * silu).astype(BF)


def route_masks(routes, weights, even, place_m, place_l, comb_m, comb_l, w_m, w_l):
    t0, t1 = iota((128, 128), 0), iota((128, 128), 1)
    eye = t0 == t1
    ids = routes[...].astype(F32)
    row = [ids[k:k + 1, :] for k in range(2)]
    col = [jnp.sum(jnp.where(eye, r, 0.0), axis=1, keepdims=True) for r in row]

    def count(same, ahead, axis):
        n = sum(jnp.where(s & ahead, 1.0, 0.0) for s in same)
        return jnp.sum(n, axis=axis, keepdims=True)

    row_rank = [count([c == r for c in col], t0 < t1, 0) for r in row]
    col_rank = [count([r == c for r in row], t1 < t0, 1) for c in col]

    def slots(ids, ranks):
        main = [jnp.where(k < 16, e * 16 + k, -1.0) for e, k in zip(ids, ranks)]
        rest = [jnp.where(k >= 16, e * 4 + k - 16, -1.0) for e, k in zip(ids, ranks)]
        return main, rest

    def fill(place, w, hits, slot):
        masks = [h == slot for h in hits]
        place[...] = onehot(masks[0] | masks[1])
        picked = sum(jnp.where(mk, weights[k:k + 1, :], 0.0) for k, mk in enumerate(masks))
        picked = jnp.sum(picked, axis=1, keepdims=True)
        w[...] = jnp.where(even, jnp.ones_like(picked), picked)

    main, rest = slots(row, row_rank)
    s = iota((256, 128), 0)
    fill(place_m, w_m, main, s.astype(F32))
    fill(place_l, w_l, rest, ((s >> 4) * 4 + (s & 3)).astype(F32))
    main, rest = slots(col, col_rank)
    s = iota((128, 256), 1)
    sf, sl = s.astype(F32), ((s >> 4) * 4 + (s & 3)).astype(F32)
    comb_m[...] = onehot((main[0] == sf) | (main[1] == sf))
    comb_l[...] = onehot((rest[0] == sl) | (rest[1] == sl))


def kernel(
    tok_in, cot_in, routes_in, weights_in, dg_in, du_in, dd_in, eg_in, eu_in, ed_in,
    out_x, out_g, out_u, out_d,
    tok, cot, routes, weights, dg, du, dd, eg, eu, ed, res, place_m, place_l, comb_m, comb_l, w_m, w_l, unfold, fold, wblk, blk,
    packed, shards, lbuf, wall, sib_w, acc, accl, grm, grl, hm, hl, sib_m, sib_l,
    tr, fsend, frecv, xt, ggt, dense, own_sum, rs_send, rs_recv,
    c_s, c_r, d_s, d_r, m_s, m_r, b_s, b_r, bm_s, bm_r, w_s, w_r,
    g_s, g_r, f_s, f_r, a_s, a_r, r_s, r_r, loc,
):
    i = lax.axis_index("expert")
    z = lax.axis_index("tensor")
    c = lax.rem(i, 2)
    j = lax.div(i, 2)
    y, x = lax.div(j, 4), lax.rem(j, 4)
    sib = i + 1 - 2 * c
    par = lax.rem(z, 2)
    even = par == 0
    first = (1 - c) * x + c * y
    second = (1 - c) * y + c * x

    def plane(f, s):
        yy = (1 - c) * s + c * f
        xx = (1 - c) * f + c * s
        return ((yy * 4 + xx) * 2 + c, z)

    def shifted(v, s, n):
        return lax.rem(v + s + n, n)

    pending = []

    def send(src, dst, s_sem, r_sem, n, dev):
        copy = pltpu.make_async_remote_copy(
            src_ref=src, dst_ref=dst, send_sem=s_sem.at[n], recv_sem=r_sem.at[n],
            device_id=dev, device_id_type=MESH,
        )
        copy.start()
        pending.append(copy)

    def arrived(ref, s_sem, r_sem, n):
        pltpu.make_async_remote_copy(
            src_ref=ref, dst_ref=ref, send_sem=s_sem.at[0], recv_sem=r_sem.at[n],
            device_id=(sib, z), device_id_type=MESH,
        ).wait_recv()

    def local(src, dst, n):
        copy = pltpu.make_async_copy(src, dst, loc.at[n])
        copy.start()
        return copy

    offsets = ((0, 0), (1, 1), (3, 3), (1, 3), (3, 1), (2, 0), (0, 2), (2, 2),
               (1, 0), (0, 1), (3, 0), (0, 3), (2, 1), (1, 2), (2, 3), (3, 2))

    def chip(k, sign=1):
        p, q = ((sign * v) % 4 for v in offsets[k])
        return (lax.rem(y + (1 - c) * q + c * p, 4) * 4 + lax.rem(x + (1 - c) * p + c * q, 4))

    barrier = pltpu.get_barrier_semaphore()
    for k in range(1, 16):
        pl.semaphore_signal(barrier, inc=1, device_id=(chip(k) * 2 + c, z), device_id_type=MESH)
    pl.semaphore_signal(barrier, inc=1, device_id=(sib, z), device_id_type=MESH)
    for s in range(1, 8):
        pl.semaphore_signal(barrier, inc=1, device_id=(i, shifted(z, s, 8)), device_id_type=MESH)
    early = [local(src, dst, 12 + n) for n, (src, dst) in enumerate((
        (tok_in, tok), (cot_in, cot), (dg_in, dg), (du_in, du), (dd_in, dd),
        (routes_in, routes), (weights_in, weights)))]
    loads = [local(eg_in, eg, 0), local(eu_in, eu, 1), local(ed_in, ed, 2)]
    for copy in early:
        copy.wait()

    xt[z, :, 0:128] = tok[...]
    xt[z, :, 128:256] = cot[...]
    at, k_ = iota((64, ROWS), 0), iota((64, ROWS), 1)
    wblk[...] = sum(
        dot(onehot(at == k_ + ROWS * n), m[0]) for n, m in enumerate((dg, du, dd))).astype(BF)
    pl.semaphore_wait(barrier, 23)

    right, left_z = shifted(z, 1, 8), shifted(z, -1, 8)

    def lanes(o, n):
        return xt.at[o, :, pl.ds(pl.multiple_of(128 * n, 128), 128)]

    def xt_half(o, h):
        return xt.at[o, pl.ds(224 * h, 224), :]

    for n, lane in enumerate((1 - par, par)):
        send(lanes(z, lane), lanes(z, lane), a_s, a_r, n, (i, right))
        send(lanes(z, lane), lanes(z, lane), a_s, a_r, 5 + n, (i, left_z))

    def ring_step(s):
        for base, sign, dev in ((0, -1, (i, right)), (5, 1, (i, left_z))):
            o = shifted(z, sign * s, 8)
            if s == 1:
                arrived(lanes(o, 1 - par), a_s, a_r, base + 1)
            else:
                arrived(xt.at[o], a_s, a_r, base + s)
            part = xt.at[o] if s < 3 else xt_half(o, 0 if base == 0 else 1)
            send(part, part, a_s, a_r, base + s + 1, dev)

    def ring_end():
        o = shifted(z, 4, 8)
        arrived(xt_half(o, 0), a_s, a_r, 4)
        arrived(xt_half(o, 1), a_s, a_r, 9)

    def block(pos, h):
        return wall.at[c, pos, pl.ds(32 * h, 32), :]

    own_pos = second * 4 + first
    here = local(wblk, wall.at[c, own_pos], 3)
    send(wblk, wall.at[c, own_pos], b_s, b_r, 0, plane(shifted(first, 1, 4), second))
    send(wblk, wall.at[c, own_pos], b_s, b_r, 1, plane(shifted(first, -1, 4), second))

    route_masks(routes, weights, even, place_m, place_l, comb_m, comb_l, w_m, w_l)
    r, k_ = iota((256, 256), 0), iota((256, 256), 1)
    unfold[...] = onehot(k_ == ((r >> 2) & 15) * 16 + (r >> 6) * 4 + (r & 3))
    r, k_ = iota((128, 128), 0), iota((128, 128), 1)
    fold[...] = onehot(r == ((k_ >> 2) & 7) * 16 + (k_ >> 5) * 4 + (k_ & 3))
    acc[...] = jnp.zeros_like(acc)
    accl[...] = jnp.zeros_like(accl)

    eye128 = onehot(iota((128, 128), 0) == iota((128, 128), 1))
    pair = lax.div(z, 2)
    arrived(lanes(shifted(z, -1, 8), par), a_s, a_r, 0)
    arrived(lanes(shifted(z, 1, 8), par), a_s, a_r, 5)
    for h in range(2):
        blk[448 * h:448 * h + 448, :] = xt[2 * pair + h, :, pl.ds(pl.multiple_of(128 * par, 128), 128)]

    packed[:, 0:PAIR] = (dot(place_m[...], blk[...], NT) * w_m[...]).astype(BF)
    quarter = (iota((256, 128), 0) >> 2) & 3
    sel = [jnp.where(quarter == q, place_l[...], jnp.zeros((256, 128), BF)) for q in range(4)]
    left = [sum(dot(sel[q], blk[256 * q + 128 * h:256 * q + 128 * h + 128, :], NT)
                for q in range(4) if 256 * q + 128 * h < PAIR) for h in range(2)]
    for h in range(2):
        packed[:, PAIR + 128 * h:PAIR + 128 * h + 128] = (left[h] * w_l[...]).astype(BF)

    def rows16(ref, n):
        return ref.at[pl.ds(pl.multiple_of(16 * n, 16), 16), :]

    def own_rows(k):
        return shards.at[z, k // 8, c, pl.ds(16 * (k % 8), 16), :]

    for k in range(1, 16):
        to = chip(k)
        send(rows16(packed, to), own_rows(k), c_s, c_r, k, (to * 2 + c, z))
    keep = local(rows16(packed, j), own_rows(0), 4)
    here.wait()
    send(wall.at[c, own_pos], wall.at[c, own_pos], bm_s, bm_r, 0, (sib, z))
    for copy in loads:
        copy.wait()
    send(eg, sib_w.at[0], w_s, w_r, 0, (sib, z))
    send(eu, sib_w.at[1], w_s, w_r, 1, (sib, z))

    before = second * 4 + shifted(first, -1, 4)
    after = second * 4 + shifted(first, 1, 4)
    across = second * 4 + shifted(first, 2, 4)
    arrived(wall.at[c, before], b_s, b_r, 0)
    send(block(before, 0), block(before, 0), b_s, b_r, 2, plane(shifted(first, 1, 4), second))
    arrived(wall.at[c, after], b_s, b_r, 1)
    send(block(after, 1), block(after, 1), b_s, b_r, 3, plane(shifted(first, -1, 4), second))
    ring_step(1)

    def shard(o, h):
        return shards.at[o, h, c]

    def shard_part(o, h, p):
        return shards.at[o, h, c, pl.ds(64 * p, 64), :]

    def mirror(s, h):
        o = shifted(z, s, 8)
        send(shard(o, h), shard(o, h), m_s, m_r, 2 * s + h, (sib, z))

    def hop(s, h):
        for base, sign, dev in ((8 * h, -1, (i, right)), (8 * h + 4, 1, (i, left_z))):
            o = shifted(z, sign * s, 8)
            if s:
                arrived(shard(o, h), d_s, d_r, base + s - 1)
            part = shard(o, h) if s < 3 else shard_part(o, h, 0 if sign < 0 else 1)
            send(part, part, d_s, d_r, base + s, dev)
        if s:
            mirror(s, h)
            mirror(8 - s, h)

    def hop_end(h):
        o = shifted(z, 4, 8)
        arrived(shard_part(o, h, 0), d_s, d_r, 8 * h + 3)
        arrived(shard_part(o, h, 1), d_s, d_r, 8 * h + 7)
        mirror(4, h)

    keep.wait()
    for k in range(1, 8):
        arrived(own_rows(k), c_s, c_r, k)
    hop(0, 0)
    for k in range(8, 16):
        arrived(own_rows(k), c_s, c_r, k)

    def group(g):
        return wall.at[c, pl.ds(g * 4, 4)]

    def group_half(g, h):
        return wall.at[c, pl.ds(g * 4 + 2 * h, 2)]

    arrived(block(across, 0), b_s, b_r, 2)
    arrived(block(across, 1), b_s, b_r, 3)
    s_up, s_down, s_over = (shifted(second, 1, 4), shifted(second, -1, 4), shifted(second, 2, 4))
    send(group(second), group(second), b_s, b_r, 4, plane(first, s_up))
    send(group(second), group(second), b_s, b_r, 5, plane(first, s_down))
    mirror(0, 0)
    mirror(0, 1)
    send(wall.at[c, before], wall.at[c, before], bm_s, bm_r, 1, (sib, z))
    send(wall.at[c, after], wall.at[c, after], bm_s, bm_r, 2, (sib, z))
    send(wall.at[c, across], wall.at[c, across], bm_s, bm_r, 3, (sib, z))

    def absorb(s, h):
        o = shifted(z, s, 8)
        arrived(shards.at[o, h, 1 - c], m_s, m_r, 2 * s + h)
        base = lax.div(o, 2) * PAIR
        cols = pl.ds(pl.multiple_of(base, 128), PAIR)
        arr = lax.rem(o, 2)
        flat = dot(unfold[...], shards[o, h, :, :, PAIR:WIDE].reshape(256, 256)).astype(BF)
        for q in range(4):
            n = 256 if q < 3 else 128
            lbuf[arr, 64 * h:64 * h + 64, pl.ds(pl.multiple_of(base + 256 * q, 128), n)] = (
                flat[64 * q:64 * q + 64, 0:n])

        def add(n, w):
            wc = w[:, cols]
            acc[n, h] += dot(wc, shards[o, h, :, :, 0:PAIR].reshape(256, PAIR), NT)
            accl[n, h] += dot(wc, lbuf[arr, 64 * h:64 * h + 64, cols], NT)

        @pl.when(arr == 0)
        def _():
            add(0, eg)
            add(1, eu)

        @pl.when(arr == 1)
        def _():
            add(2, ed)

    o_c = 1 - c
    sib_f = c * x + (1 - c) * y
    sib_s = c * y + (1 - c) * x

    def dense_forward(cc, g):
        w = wall[cc, pl.ds(g * 4, 4)].reshape(256, 3584)
        p = dot(w, xt[...].reshape(3584, 256))
        gate = p[:, 0:128]
        up = pltpu.roll(gate, 256 - ROWS, 0)
        grad = pltpu.roll(p[:, 128:256], 256 - 2 * ROWS, 0)
        _, gg, gu = swiglu(gate, up, grad)
        row = iota((256, 128), 0) & 63
        shift = pltpu.roll(gu.astype(F32), ROWS, 0)
        both = jnp.where(row < ROWS, gg.astype(F32), jnp.where(row < 2 * ROWS, shift, 0.0)).astype(BF)
        ggt[cc * 4 + g] = dot(eye128, both, NT).astype(BF)

    def dense_back(n, carry):
        cols = pl.ds(pl.multiple_of(n * 512, 128), 512)
        dense[:, cols] = sum(
            dot(ggt[k], wall[k // 4, 4 * (k % 4):4 * (k % 4) + 4, :, cols].reshape(256, 512))
            for k in range(8))
        return carry

    def hidden(h):
        silu, gg, gu = swiglu(acc[0, h], acc[1, h], acc[2, h])
        hm[h] = (silu * acc[1, h]).astype(BF)
        grm[h, 0] = gg
        grm[h, 1] = gu
        send(grm.at[h], sib_m.at[h], g_s, g_r, 2 * h, (sib, z))
        silu, gg, gu = swiglu(accl[0, h], accl[1, h], accl[2, h])
        hl[h] = (silu * accl[1, h]).astype(BF)
        grl[h, 0] = gg
        grl[h, 1] = gu
        send(grl.at[h], sib_l.at[h], g_s, g_r, 2 * h + 1, (sib, z))

    chunk = [shifted(pair, 2, 4), shifted(pair, 1 - 2 * par, 4), shifted(pair, 2 * par - 1, 4), pair]
    keeps = []

    def give_back(h):
        pick_m = onehot(iota((128, 256), 1) == iota((128, 256), 0) + 128 * c)
        pick_l = onehot(iota((32, 64), 1) == iota((32, 64), 0) + 32 * c)
        for n in range(2):
            tr[n, 0:128, :] = dot(pick_m, grm[h, n], NT).astype(BF)
            tr[n, 128:160, :] = dot(pick_l, grl[h, n], NT).astype(BF)
        arrived(sib_m.at[h], g_s, g_r, 2 * h)
        arrived(sib_l.at[h], g_s, g_r, 2 * h + 1)
        for n in range(2):
            tr[2 + n, 0:128, :] = dot(pick_m, sib_m[h, n], NT).astype(BF)
            tr[2 + n, 128:160, :] = dot(pick_l, sib_l[h, n], NT).astype(BF)
        for k in range(4):
            cols = pl.ds(pl.multiple_of(chunk[k] * PAIR, 128), PAIR)
            o = (dot(tr[0], eg[:, cols]) + dot(tr[1], eu[:, cols])
                 + dot(tr[2], sib_w[0, :, cols]) + dot(tr[3], sib_w[1, :, cols])).astype(BF)
            fsend[h, k, :, 0:PAIR] = o[0:128]
            tail = o[128:160]
            stack = jnp.concatenate(
                [tail[:, 0:256], tail[:, 256:512], tail[:, 512:768],
                 jnp.concatenate([tail[:, 768:896], jnp.zeros((32, 128), BF)], axis=1)], axis=0)
            fsend[h, k, :, PAIR:WIDE] = dot(fold[...], stack).astype(BF)
            for n in range(8):
                src, dst = fsend.at[h, k, pl.ds(16 * n, 16), :], rows16(frecv.at[k], j)
                if h or n:
                    send(src, dst, f_s, f_r, 16 * k + 8 * h + n, (chip(8 * h + n, -1) * 2 + c, z))
                else:
                    keeps.append(local(src, dst, 5 + k))

    absorb(0, 0)
    hop(1, 0)
    absorb(1, 0)
    absorb(7, 0)
    absorb(0, 1)
    hop(2, 0)
    ring_step(2)
    absorb(2, 0)
    absorb(6, 0)
    hop(3, 0)
    hop(0, 1)
    absorb(3, 0)
    absorb(5, 0)
    arrived(group(s_down), b_s, b_r, 4)
    send(group_half(s_down, 0), group_half(s_down, 0), b_s, b_r, 6, plane(first, s_up))
    send(group(s_down), group(s_down), bm_s, bm_r, 4, (sib, z))
    arrived(group(s_up), b_s, b_r, 5)
    send(group_half(s_up, 1), group_half(s_up, 1), b_s, b_r, 7, plane(first, s_down))
    send(group(s_up), group(s_up), bm_s, bm_r, 5, (sib, z))
    hop_end(0)
    ring_step(3)
    absorb(4, 0)
    hidden(0)
    arrived(sib_w.at[0], w_s, w_r, 0)
    arrived(sib_w.at[1], w_s, w_r, 1)
    hop(1, 1)
    give_back(0)
    hop(2, 1)
    absorb(1, 1)
    absorb(7, 1)
    arrived(group_half(s_over, 0), b_s, b_r, 6)
    arrived(group_half(s_over, 1), b_s, b_r, 7)
    send(group(s_over), group(s_over), bm_s, bm_r, 6, (sib, z))
    ring_end()
    for n, f in enumerate((0, -1, 1, 2)):
        arrived(wall.at[o_c, sib_s * 4 + shifted(sib_f, f, 4)], bm_s, bm_r, n)
    dense_forward(c, second)
    dense_forward(o_c, sib_s)
    dense_forward(c, s_down)
    dense_forward(c, s_up)
    absorb(2, 1)
    absorb(6, 1)
    hop(3, 1)
    for n, s in enumerate((-1, 1)):
        g = shifted(sib_s, s, 4)
        arrived(wall.at[o_c, pl.ds(g * 4, 4)], bm_s, bm_r, 4 + n)
        dense_forward(o_c, g)
    absorb(3, 1)
    absorb(5, 1)
    hop_end(1)
    absorb(4, 1)
    hidden(1)
    give_back(1)

    dense_forward(c, s_over)
    g = shifted(sib_s, 2, 4)
    arrived(wall.at[o_c, pl.ds(g * 4, 4)], bm_s, bm_r, 6)
    dense_forward(o_c, g)
    lax.fori_loop(0, 7, dense_back, 0)

    outs = []

    def wgrad(n, out, g0, g1, l0, l1, arr):
        def cols_of(m, carry):
            cols = pl.ds(pl.multiple_of(m * PAIR, 128), PAIR)
            rows = [shards[2 * m + arr, h, :, :, 0:PAIR].reshape(256, PAIR) for h in range(2)]
            res[n, :, cols] = (dot(g0, rows[0]) + dot(g1, rows[1])
                               + dot(l0, lbuf[arr, 0:64, cols])
                               + dot(l1, lbuf[arr, 64:128, cols])).astype(BF)
            return carry

        lax.fori_loop(0, 4, cols_of, 0)
        outs.append(local(res.at[n], out, 9 + n))

    cq = (iota((128, 256), 1) >> 2) & 3

    def combine(k):
        for n in range(1, 16):
            arrived(rows16(frecv.at[k], chip(n)), f_s, f_r, 16 * k + n)
        keeps[k].wait()
        m = chunk[k]
        total = dense[:, pl.ds(pl.multiple_of(m * PAIR, 128), PAIR)] + dot(comb_m[...], frecv[k, :, 0:PAIR])
        parts = []
        for q in range(4):
            n = 256 if q < 3 else 128
            sel = jnp.where(cq == q, comb_l[...], jnp.zeros((128, 256), BF))
            parts.append(dot(sel, frecv[k, :, PAIR:PAIR + n]))
        total = total + jnp.concatenate(parts, axis=1)
        flip = total.T
        for h in range(2):
            own_sum[2 * m + h] = flip[448 * h:448 * h + 448]

    def reduce_step(s):
        for d, sign, dev in ((0, 1, (i, right)), (1, -1, (i, left_z))):
            to = shifted(z, sign * (5 - s), 8)
            if s == 1:
                part = pl.ds(224 * d, 224)
                rs_send[d, 0, part, :] = own_sum[to, part, :].astype(BF)
                send(rs_send.at[d, 0, part, :], rs_recv.at[d, 0, part, :], r_s, r_r, 4 * d, dev)
                continue
            got = received(d, s - 1)
            if s == 2:
                a, b = pl.ds(224 * d, 224), pl.ds(224 * (1 - d), 224)
                rs_send[d, 1, a, :] = (own_sum[to, a, :] + got).astype(BF)
                rs_send[d, 1, b, :] = own_sum[to, b, :].astype(BF)
            else:
                rs_send[d, s - 1] = (own_sum[to] + got).astype(BF)
            send(rs_send.at[d, s - 1], rs_recv.at[d, s - 1], r_s, r_r, 4 * d + s - 1, dev)

    def received(d, s):
        ref = rs_recv.at[d, 0, pl.ds(224 * d, 224), :] if s == 1 else rs_recv.at[d, s - 1]
        arrived(ref, r_s, r_r, 4 * d + s - 1)
        return ref[...].astype(F32)

    combine(0)
    reduce_step(1)
    wgrad(0, out_g, grm[0, 0], grm[1, 0], grl[0, 0], grl[1, 0], 0)
    combine(1)
    reduce_step(2)
    wgrad(1, out_u, grm[0, 1], grm[1, 1], grl[0, 1], grl[1, 1], 0)
    combine(2)
    reduce_step(3)
    combine(3)
    wgrad(2, out_d, hm[0], hm[1], hl[0], hl[1], 1)
    reduce_step(4)
    out_x[...] = (own_sum[z] + received(0, 4) + received(1, 4)).astype(BF)
    for copy in pending:
        copy.wait_send()
    for copy in outs:
        copy.wait()


def copy_out(a, b, c, d, oa, ob, oc, od, va, vb, vc, vd, sems):
    arrays = ((a, va, oa), (b, vb, ob), (c, vc, oc), (d, vd, od))
    loads = [pltpu.make_async_copy(s, v, sems.at[n]) for n, (s, v, _) in enumerate(arrays)]
    stores = [pltpu.make_async_copy(v, t, sems.at[4 + n]) for n, (_, v, t) in enumerate(arrays)]
    for copy in loads:
        copy.start()
    for load, store in zip(loads, stores):
        load.wait()
        store.start()
    for store in stores:
        store.wait()


def body(
    tokens, cotangent, routes, route_weights, dense_gate, dense_up, dense_down,
    expert_gate, expert_up, expert_down,
):
    V = pltpu.VMEM
    scratch = [
        V((448, 128), BF), V((448, 128), BF),
        V((2, 128), jnp.int32), V((2, 128), F32),
        V((1, ROWS, 3584), BF), V((1, ROWS, 3584), BF), V((1, ROWS, 3584), BF),
        V((152, 3584), BF), V((152, 3584), BF), V((152, 3584), BF),
        V((3, 152, 3584), BF),
        V((256, 128), BF), V((256, 128), BF),
        V((128, 256), BF), V((128, 256), BF),
        V((256, 1), F32), V((256, 1), F32),
        V((256, 256), BF), V((128, 128), BF),
        V((64, 3584), BF),
        V((896, 128), BF),
        V((256, WIDE), BF),
        V((8, 2, 2, 128, WIDE), BF),
        V((2, 128, 3584), BF),
        V((2, 16, 64, 3584), BF),
        V((2, 152, 3584), BF),
        V((3, 2, 152, 256), F32),
        V((3, 2, 152, 64), F32),
        V((2, 2, 152, 256), BF),
        V((2, 2, 152, 64), BF),
        V((2, 152, 256), BF),
        V((2, 152, 64), BF),
        V((2, 2, 152, 256), BF),
        V((2, 2, 152, 64), BF),
        V((4, 160, 152), BF),
        V((2, 4, 128, WIDE), BF),
        V((4, 256, WIDE), BF),
        V((8, 448, 256), BF),
        V((8, 128, 256), BF),
        V((128, 3584), F32),
        V((8, 448, 128), F32),
        V((2, 4, 448, 128), BF),
        V((2, 4, 448, 128), BF),
    ]
    for n in (16, 16, 16, 8, 7, 2, 4, 64, 10, 8):
        scratch += [pltpu.SemaphoreType.DMA((n,))] * 2
    scratch.append(pltpu.SemaphoreType.DMA((19,)))
    vm = pl.BlockSpec(memory_space=pltpu.VMEM)
    hbm = pl.BlockSpec(memory_space=pl.ANY)
    shapes = (jax.ShapeDtypeStruct((448, 128), BF),) + (jax.ShapeDtypeStruct((152, 3584), BF),) * 3
    results = pl.pallas_call(
        kernel,
        out_shape=shapes,
        in_specs=[hbm] * 10,
        out_specs=[vm] + [hbm] * 3,
        scratch_shapes=scratch,
        compiler_params=pltpu.CompilerParams(
            collective_id=0, has_side_effects=True, vmem_limit_bytes=62 * 2**20),
    )(tokens.T, cotangent.T, routes.T, route_weights.T, dense_gate, dense_up, dense_down,
      expert_gate, expert_up, expert_down)
    x, g, u, d = pl.pallas_call(
        copy_out,
        out_shape=shapes,
        in_specs=[hbm] * 4,
        out_specs=[hbm] * 4,
        scratch_shapes=[V(s.shape, BF) for s in shapes] + [pltpu.SemaphoreType.DMA((8,))],
        compiler_params=pltpu.CompilerParams(vmem_limit_bytes=62 * 2**20),
    )(*results)
    return x.T, g, u, d


def solution(mesh):
    rows = P(("expert", "tensor"), None)
    dense = P("tensor", "expert", None)
    return jax.shard_map(
        body,
        mesh=mesh,
        in_specs=(
            P("expert", "tensor"), P("expert", "tensor"), P("expert", None), P("expert", None),
            dense, dense, dense, rows, rows, rows,
        ),
        out_specs=(P("expert", "tensor"), rows, rows, rows),
        check_vma=False,
    )
```

time: 130 us -> 122 us (0.938)
  Pallas kernels: 127 us -> 119 us
    pallas_call x1, Pallas kernels: 124 us -> 116 us  [body(): pl.pallas_call(kernel, out_shape=shapes, in_specs=[hbm] * 10, out_specs=[...]
where the time goes in v3:
time: 122 us; the launch traced here: 120 us
  Pallas kernels  119 us (98%)
    pallas_call x1, Pallas kernels, body(): pl.pallas_call(kernel, out_shape=shapes, in_specs=[hbm] * 10, out_specs=[...  116 us
    pallas_call x1, Pallas kernels, body(): pl.pallas_call(copy_out, out_shape=shapes, in_specs=[hbm] * 4, out_specs=...  3.08 us

profile of v3, /device:TPU:16, one launch (start us, length us, event | category | flops | bytes accessed | tf_op | source)
XLA Modules:
  0.0 120.2 jit_solution(17271657679490979297)
XLA Ops:
  0.6 116.3 %shard_map.129 = (bf16[448,128]{1,0:T(8,128)(2,1)}, bf16[152,3584]{1,0:T(8,128)(2,1)}, bf16[152,3584]{1,0:T(8,128)(2,1)}, bf16[152,3584]{1,0:T(8,128)(2,1)}) custom-call(bf16[448,128]{1,0:T(8,128)(2,1)} %bitcast.5, bf16[448,128]{1,0:T(8,128)(2,1)} %bitcast.6, s32[2,128]{1,0:T(2,128)} %bitcast.7, f32[2,128]{1,0:T(2,128)} %bitcast.8, ...), custom_call_target="tpu_custom_call" | custom-call | tf_op jit(solution)/shard_map/pallas_call | solution.py:567
  117.0 3.1 %shard_map.130 = (bf16[448,128]{1,0:T(8,128)(2,1)}, bf16[152,3584]{1,0:T(8,128)(2,1)}, bf16[152,3584]{1,0:T(8,128)(2,1)}, bf16[152,3584]{1,0:T(8,128)(2,1)}) custom-call(bf16[448,128]{1,0:T(8,128)(2,1)} %get-tuple-element.12.a, bf16[152,3584]{1,0:T(8,128)(2,1)} %get-tuple-element.13.b, bf16[152,3584]{1,0:T(8,128)(2,1)} %get-tuple-element.14.c, ...), custom_call_target="tpu_custom_call" | custom-call | tf_op jit(solution)/shard_map/pallas_call | solution.py:577

commit v4 on v3

--- a/solution.py
+++ b/solution.py
@@ -130,7 +130,7 @@
     for k in range(1, 16):
         pl.semaphore_signal(barrier, inc=1, device_id=(chip(k) * 2 + c, z), device_id_type=MESH)
     pl.semaphore_signal(barrier, inc=1, device_id=(sib, z), device_id_type=MESH)
-    for s in range(1, 8):
+    for s in (1, -1):
         pl.semaphore_signal(barrier, inc=1, device_id=(i, shifted(z, s, 8)), device_id_type=MESH)
     early = [local(src, dst, 12 + n) for n, (src, dst) in enumerate((
         (tok_in, tok), (cot_in, cot), (dg_in, dg), (du_in, du), (dd_in, dd),
@@ -144,7 +144,7 @@
     at, k_ = iota((64, ROWS), 0), iota((64, ROWS), 1)
     wblk[...] = sum(
         dot(onehot(at == k_ + ROWS * n), m[0]) for n, m in enumerate((dg, du, dd))).astype(BF)
-    pl.semaphore_wait(barrier, 23)
+    pl.semaphore_wait(barrier, 18)
 
     right, left_z = shifted(z, 1, 8), shifted(z, -1, 8)
 
@@ -345,7 +345,7 @@
     chunk = [shifted(pair, 2, 4), shifted(pair, 1 - 2 * par, 4), shifted(pair, 2 * par - 1, 4), pair]
     keeps = []
 
-    def give_back(h):
+    def turn(h):
         pick_m = onehot(iota((128, 256), 1) == iota((128, 256), 0) + 128 * c)
         pick_l = onehot(iota((32, 64), 1) == iota((32, 64), 0) + 32 * c)
         for n in range(2):
@@ -356,7 +356,9 @@
         for n in range(2):
             tr[2 + n, 0:128, :] = dot(pick_m, sib_m[h, n], NT).astype(BF)
             tr[2 + n, 128:160, :] = dot(pick_l, sib_l[h, n], NT).astype(BF)
-        for k in range(4):
+
+    def give_back(h, ks):
+        for k in ks:
             cols = pl.ds(pl.multiple_of(chunk[k] * PAIR, 128), PAIR)
             o = (dot(tr[0], eg[:, cols]) + dot(tr[1], eu[:, cols])
                  + dot(tr[2], sib_w[0, :, cols]) + dot(tr[3], sib_w[1, :, cols])).astype(BF)
@@ -399,8 +401,10 @@
     arrived(sib_w.at[0], w_s, w_r, 0)
     arrived(sib_w.at[1], w_s, w_r, 1)
     hop(1, 1)
-    give_back(0)
+    turn(0)
+    give_back(0, (0, 1))
     hop(2, 1)
+    give_back(0, (2, 3))
     absorb(1, 1)
     absorb(7, 1)
     arrived(group_half(s_over, 0), b_s, b_r, 6)
@@ -411,22 +415,23 @@
         arrived(wall.at[o_c, sib_s * 4 + shifted(sib_f, f, 4)], bm_s, bm_r, n)
     dense_forward(c, second)
     dense_forward(o_c, sib_s)
+    hop(3, 1)
+    absorb(2, 1)
+    absorb(6, 1)
     dense_forward(c, s_down)
     dense_forward(c, s_up)
-    absorb(2, 1)
-    absorb(6, 1)
-    hop(3, 1)
-    for n, s in enumerate((-1, 1)):
-        g = shifted(sib_s, s, 4)
-        arrived(wall.at[o_c, pl.ds(g * 4, 4)], bm_s, bm_r, 4 + n)
-        dense_forward(o_c, g)
     absorb(3, 1)
     absorb(5, 1)
     hop_end(1)
     absorb(4, 1)
     hidden(1)
-    give_back(1)
-
+    turn(1)
+    give_back(1, range(4))
+
+    for n, s in enumerate((-1, 1)):
+        g = shifted(sib_s, s, 4)
+        arrived(wall.at[o_c, pl.ds(g * 4, 4)], bm_s, bm_r, 4 + n)
+        dense_forward(o_c, g)
     dense_forward(c, s_over)
     g = shifted(sib_s, 2, 4)
     arrived(wall.at[o_c, pl.ds(g * 4, 4)], bm_s, bm_r, 6)
@@ -496,11 +501,11 @@
     combine(2)
     reduce_step(3)
     combine(3)
+    reduce_step(4)
     wgrad(2, out_d, hm[0], hm[1], hl[0], hl[1], 1)
-    reduce_step(4)
-    out_x[...] = (own_sum[z] + received(0, 4) + received(1, 4)).astype(BF)
     for copy in pending:
         copy.wait_send()
+    out_x[...] = (own_sum[z] + received(0, 4) + received(1, 4)).astype(BF)
     for copy in outs:
         copy.wait()
 

time: 122 us -> 119 us (0.975); the launches traced: 120 us -> 119 us
    pallas_call x1, Pallas kernels: 116 us -> 115 us  [body(): pl.pallas_call(kernel, out_shape=shapes, in_specs=[hbm] * 10, out_specs=[...]
where the time goes in v4:
time: 119 us
  Pallas kernels  118 us (99%)
    pallas_call x1, Pallas kernels, body(): pl.pallas_call(kernel, out_shape=shapes, in_specs=[hbm] * 10, out_specs=[...  115 us
    pallas_call x1, Pallas kernels, body(): pl.pallas_call(copy_out, out_shape=shapes, in_specs=[hbm] * 4, out_specs=...  3.08 us

profile of v4, /device:TPU:16, one launch (start us, length us, event | category | flops | bytes accessed | tf_op | source)
XLA Modules:
  0.0 118.5 jit_solution(2733781204024200190)
XLA Ops:
  0.6 114.7 %shard_map.129 = (bf16[448,128]{1,0:T(8,128)(2,1)}, bf16[152,3584]{1,0:T(8,128)(2,1)}, bf16[152,3584]{1,0:T(8,128)(2,1)}, bf16[152,3584]{1,0:T(8,128)(2,1)}) custom-call(bf16[448,128]{1,0:T(8,128)(2,1)} %bitcast.5, bf16[448,128]{1,0:T(8,128)(2,1)} %bitcast.6, s32[2,128]{1,0:T(2,128)} %bitcast.7, f32[2,128]{1,0:T(2,128)} %bitcast.8, ...), custom_call_target="tpu_custom_call" | custom-call | tf_op jit(solution)/shard_map/pallas_call | solution.py:572
  115.3 3.1 %shard_map.130 = (bf16[448,128]{1,0:T(8,128)(2,1)}, bf16[152,3584]{1,0:T(8,128)(2,1)}, bf16[152,3584]{1,0:T(8,128)(2,1)}, bf16[152,3584]{1,0:T(8,128)(2,1)}) custom-call(bf16[448,128]{1,0:T(8,128)(2,1)} %get-tuple-element.12.a, bf16[152,3584]{1,0:T(8,128)(2,1)} %get-tuple-element.13.b, bf16[152,3584]{1,0:T(8,128)(2,1)} %get-tuple-element.14.c, ...), custom_call_target="tpu_custom_call" | custom-call | tf_op jit(solution)/shard_map/pallas_call | solution.py:582
